TPU v7x, 128 devices: a whole 4x4x4 slice. The times are simulated.
128 devices in a mesh: row: 4 (over z), col: 32 (over x, y, core).
Axes of the slice: x: 4, y: 4, z: 4, core: 2. Of those that a mesh axis runs over, the one named last changes fastest.
Arguments:
- layer_input: bfloat16 [1088, 16384], P('col', 'row'), may hold values from -6 to 6
- cotangent: bfloat16 [1088, 16384], P('col', 'row'), may hold values from -6 to 6
- segments: int32 [16, 1024], P('row'), may hold values from 0 to 3, as said below
- qkv_weight: bfloat16 [1088, 3, 1088], P('row', None, 'col'), may hold values from -0.1875 to 0.1875
- qv_bias: bfloat16 [2, 1088], P(None, 'col'), may hold values from -1 to 1
- out_weight: bfloat16 [1088, 1088], P('row', 'col'), may hold values from -1.5 to 1.5
- out_bias: bfloat16 [1088], P('col'), may hold values from -1 to 1
- up_weight: bfloat16 [1088, 4352], P('row', 'col'), may hold values from -0.1875 to 0.1875
- up_bias: bfloat16 [4352], P('col'), may hold values from -1 to 1
- down_weight: bfloat16 [4352, 1088], P('col', 'row'), may hold values from -0.09375 to 0.09375
- down_bias: bfloat16 [1088], P('col'), may hold values from -1 to 1
- first_gain: bfloat16 [1088], P('col'), may hold values from 0.5 to 1.5
- first_shift: bfloat16 [1088], P('col'), may hold values from -1 to 1
- second_gain: bfloat16 [1088], P('col'), may hold values from 0.5 to 1.5
- second_shift: bfloat16 [1088], P('col'), may hold values from -1 to 1
Outputs:
- layer_output: float32 [1088, 16384], P('col', 'row')
- input_grad: float32 [1088, 16384], P('col', 'row')
- qkv_grad: float32 [1088, 3, 1088], P('row', None, 'col')
- qvbias_grad: float32 [2, 1088], P(None, 'col')
- out_grad: float32 [1088, 1088], P('row', 'col')
- outbias_grad: float32 [1088], P('col')
- up_grad: float32 [1088, 4352], P('row', 'col')
- upbias_grad: float32 [4352], P('col')
- down_grad: float32 [4352, 1088], P('col', 'row')
- downbias_grad: float32 [1088], P('col')
- firstgain_grad: float32 [1088], P('col')
- firstshift_grad: float32 [1088], P('col')
- secondgain_grad: float32 [1088], P('col')
- secondshift_grad: float32 [1088], P('col')
Inputs may be any that keep to these rules, and one draw needn't show every extreme that they name: `segments`: segment numbers never fall along a sequence. In each row index's 4 sequences one sequence is a single document.
All inputs are finite; a program needn't handle non-finite values.
Results may differ from a plain program's by a relative error of at most 0.014.
Values may be sent and summed in bfloat16 or wider, within the bound.
A program may use at most 256 MiB of HBM per device.

v0:
```python
import jax
import jax.numpy as jnp
from jax import lax
from jax.experimental import pallas as pl
from jax.experimental.pallas import tpu as pltpu
from jax.sharding import Mesh, PartitionSpec as P

HEADS = 17
HD = 64
EPS = 1e-05
XY = ("x", "y")
COL = ("x", "y", "core")
F32 = jnp.float32
BF16 = jnp.bfloat16
QB = 256


def nn(a, b):
    return lax.dot_general(a, b, (((1,), (0,)), ((), ())), preferred_element_type=F32)


def nt(a, b):
    return lax.dot_general(a, b, (((1,), (1,)), ((), ())), preferred_element_type=F32)


MESH = pl.DeviceIdType.MESH
ANY = pl.BlockSpec(memory_space=pl.ANY)
VMEM = pl.BlockSpec(memory_space=pltpu.VMEM)
DMA = pltpu.SemaphoreType.DMA


def params(collective_id, vmem=56):
    return pltpu.CompilerParams(
        collective_id=collective_id, has_side_effects=True, vmem_limit_bytes=vmem * 2**20
    )


def remote(src, dst, send_sem, recv_sem, where):
    return pltpu.make_async_remote_copy(
        src_ref=src,
        dst_ref=dst,
        send_sem=send_sem,
        recv_sem=recv_sem,
        device_id=where,
        device_id_type=MESH,
    )


def signal(where):
    pl.semaphore_signal(
        pltpu.get_barrier_semaphore(), inc=1, device_id=where, device_id_type=MESH
    )


def col_place():
    return (lax.axis_index("x") * 4 + lax.axis_index("y")) * 2 + lax.axis_index("core")


def col_device(place):
    return {"x": place // 8, "y": place // 2 % 4, "core": place % 2}


def greet_col():
    me = col_place()

    def greet(step, _):
        signal(col_device((me + step) % 32))
        return 0

    lax.fori_loop(1, 32, greet, 0)
    return me


def rows_of(n):
    return pl.ds(pl.multiple_of(n, 256), 256)


def token_swap(src, out, send, recv, local, me):
    def copy(step, owner):
        peer = (me + step) % 32
        return remote(
            src.at[:, rows_of(peer // 2 * 256)], out.at[owner], send.at[step], recv.at[step], col_device(peer)
        )

    own = pltpu.make_async_copy(src.at[:, rows_of(me // 2 * 256)], out.at[me], local)

    def begin():
        def one(step, _):
            copy(step, me).start()
            return 0

        lax.fori_loop(1, 32, one, 0)
        own.start()

    def end():
        def one(step, _):
            copy(step, (me + 32 - step) % 32).wait()
            return 0

        lax.fori_loop(1, 32, one, 0)
        own.wait()

    return begin, end


def ring(axis, step):
    return {axis: (lax.axis_index(axis) + 4 + step) % 4}


QKV_ROWS, OUT_ROWS, FF_ROWS = 112, 48, 144
ATTN_ROWS = QKV_ROWS + OUT_ROWS
ATTN_FLOWS = ((0, 0, 32, 16, 0), (1, 0, 48, 16, 0), (0, 32, 80, 32, 1))
UP_FLOWS = ((0, 0, 64, 32, 0), (0, 64, 80, 32, 1))
DOWN_FLOWS = ((0, 0, 160, 80, 1),)
DOWN_ROWS, DOWN_MAIN = 160, 256
FIRST_FLOWS = ((0, 0, 48, 16, 0), (1, 0, 48, 16, 0), (1, 48, 96, 48, 1))
LAST_FLOWS = ((0, 0, 48, 16, 0), (0, 48, 64, 32, 1))
COLUMN_FLOWS = ((0, 0, 48, 16, 0),)
WIDE, WINDOW, LANE = 1152, 384, 128
SUM_ROWS = (OUT_ROWS, FF_ROWS, QKV_ROWS)
SUM_FIRST = (0, 48, 192)


def ring_gather(flows, blocks, place, send, recv, stages=2):
    ix, iy, iz = (lax.axis_index(a) for a in ("x", "y", "row"))
    every = range(len(flows))

    def axis_of(flow, stage):
        return "row" if stage == 2 else "xy"[(flows[flow][4] + stage) % 2]

    def region(flow, stage, owner, half=None):
        by_x = axis_of(flow, stage) == "x"
        slab, first, count, cut, _ = flows[flow]
        if stage == 0:
            row, rows = ((0, count), (0, cut), (cut, count - cut))[0 if half is None else half + 1]
            return place(slab, owner if by_x else ix, iy if by_x else owner, pl.ds(first + row, rows), iz)
        part = pl.ds(0, 4) if half is None else pl.ds(2 * half, 2)
        if stage == 2:
            return place(slab, part, pl.ds(0, 4), pl.ds(first, count), owner)
        return place(slab, owner if by_x else part, part if by_x else owner, pl.ds(first, count), iz)

    def copy(flow, stage, kind, owner):
        half = None if kind < 2 else kind - 2
        there = region(flow, stage, owner, half)
        if stage == 0 and kind < 2:
            slab, first, count, _, _ = flows[flow]
            here = blocks[slab].at[pl.ds(first, count)]
        else:
            here = there
        return remote(
            here,
            there,
            send.at[flow, stage, kind],
            recv.at[flow, stage, kind],
            ring(axis_of(flow, stage), 1 if kind % 2 == 0 else -1),
        )

    def at(flow, stage, step):
        return (lax.axis_index(axis_of(flow, stage)) + 4 + step) % 4

    def begin(stage):
        for flow in every:
            for kind in (0, 1):
                copy(flow, stage, kind, at(flow, stage, 0)).start()

    def middle(stage, then=None):
        for flow in every:
            for kind, step in ((0, -1), (1, 1)):
                owner = at(flow, stage, step)
                copy(flow, stage, kind, owner).wait_recv()
                copy(flow, stage, kind + 2, owner).start()
                if then is not None:
                    then(flow, 1 + kind, owner)

    def finish(stage, then=None):
        for flow in every:
            owner = at(flow, stage, 2)
            for kind in (2, 3):
                copy(flow, stage, kind, owner).wait_recv()
            if then is not None:
                then(flow, 3, owner)

    def end():
        for stage in range(stages):
            for flow in every:
                for kind in range(4):
                    copy(flow, stage, kind, at(flow, stage, 0)).wait_send()

    return begin, middle, finish, end, at


def lay_out(source, quad, target, lanes=slice(None)):
    def one(step, _):
        for part in range(4):
            quad[34 * part : 34 * part + 34] = source(step * 4 + part)
        target[pl.ds(pl.multiple_of(step * 136, 8), 136)] = quad[...].astype(target.dtype)
        return 0

    lax.fori_loop(0, 8, one, 0)


def norm_in(v, gain, shift):
    centred = v - jnp.mean(v, 0, keepdims=True)
    inv_std = lax.rsqrt(jnp.mean(centred * centred, 0, keepdims=True) + EPS)
    standard = centred * inv_std
    return (standard * gain + shift).astype(BF16), standard, inv_std


def add_rows(out, *terms):
    def one(i, _):
        out[i] = sum(t[i].astype(F32) for t in terms).astype(out.dtype)
        return 0

    lax.fori_loop(0, out.shape[0], one, 0)


def ring_reduce(flows, ins, outs, bufs, send, recv, by_z=False):
    every = range(len(flows))
    stages = 3 if by_z else 2

    def axis_of(flow, stage):
        return ("row", "x", "y")[stage] if by_z else "yx"[(flows[flow][4] + stage) % 2]

    def at(flow, stage, step):
        return (lax.axis_index(axis_of(flow, stage)) + 4 + step) % 4

    def held(flow, stage):
        first = (flow * stages + stage) * 4
        return bufs[first : first + 4]

    def chunk(flow, stage, owner, half=None):
        slab, first, count, cut, _ = flows[flow]
        if stage == stages - 1:
            row, rows = ((0, count), (0, cut), (cut, count - cut))[0 if half is None else half + 1]
            return held(flow, stage - 1)[2].at[pl.ds(owner, 1), pl.ds(row, rows)]
        if stage == 1:
            return held(flow, 0)[2].at[pl.ds(owner * 4, 4) if half is None else pl.ds(owner * 4 + 2 * half, 2)]
        window = pl.ds(first, count)
        ref = ins[slab]
        if by_z:
            return ref.at[owner, pl.ds(0, 16) if half is None else pl.ds(8 * half, 8), window]
        part = pl.ds(0, 4) if half is None else pl.ds(2 * half, 2)
        return ref.at[part, owner, window] if axis_of(flow, 0) == "y" else ref.at[owner, part, window]

    def part_of(flow, stage, ref, half):
        if stage < stages - 1:
            count = ref.shape[0] // 2
            return ref.at[pl.ds(count * half, count)]
        _, _, count, cut, _ = flows[flow]
        return ref.at[:, pl.ds(0, cut) if half == 0 else pl.ds(cut, count - cut)]

    def copy(flow, stage, kind):
        from_left, from_right, all_left, all_right = held(flow, stage)
        right = kind % 2 == 0
        if kind < 2:
            src, dst = chunk(flow, stage, at(flow, stage, 2), kind), (from_left, from_right)[kind]
        elif kind < 4:
            src = chunk(flow, stage, at(flow, stage, 1 if right else -1), 1 if right else 0)
            dst = part_of(flow, stage, all_left if right else all_right, 1 if right else 0)
        else:
            src = from_left if right else from_right
            dst = part_of(flow, stage, all_left if right else all_right, 0 if right else 1)
        return remote(
            src,
            dst,
            send.at[flow, stage, kind],
            recv.at[flow, stage, kind],
            ring(axis_of(flow, stage), 1 if right else -1),
        )

    def begin(stage, kinds=(0, 1, 2, 3)):
        for kind in kinds:
            for flow in every:
                copy(flow, stage, kind).start()

    def middle(stage):
        for flow in every:
            from_left, from_right = held(flow, stage)[:2]
            for kind, buf, step in ((0, from_left, 1), (1, from_right, -1)):
                copy(flow, stage, kind).wait_recv()
                add_rows(buf, buf, chunk(flow, stage, at(flow, stage, step), kind))
                copy(flow, stage, kind + 4).start()

    def finish(stage):
        for flow in every:
            all_left, all_right = held(flow, stage)[2:4]
            for kind in (2, 3, 4, 5):
                copy(flow, stage, kind).wait_recv()
            out = all_left
            if stage == stages - 1:
                slab, first, count, _, _ = flows[flow]
                out = outs[slab].at[:, pl.ds(first, count)]
            add_rows(out, chunk(flow, stage, at(flow, stage, 0)), all_left, all_right)

    def end():
        for stage in range(stages):
            for flow in every:
                for kind in range(6):
                    copy(flow, stage, kind).wait_send()

    return begin, middle, finish, end


def ring_bufs(flows, columns, by_z=False):
    stages = 3 if by_z else 2
    bufs = []
    for _, _, count, cut, _ in flows:
        for n in (16, 4) if by_z else (4,):
            bufs += [(n // 2, count), (n // 2, count), (n, count), (n, count)]
        bufs += [(1, cut), (1, count - cut), (1, count), (1, count)]
    sems = [DMA((len(flows), stages, 6)), DMA((len(flows), stages, 6))]
    return sems, [pltpu.VMEM((n, rows, columns), BF16) for n, rows in bufs]


def core_kernel(mine, total, got, send, recv):
    partner = {"core": 1 - lax.axis_index("core")}
    signal(partner)
    pl.semaphore_wait(pltpu.get_barrier_semaphore(), 1)
    copy = remote(mine, got, send, recv, partner)
    copy.start()
    copy.wait()
    total[...] = mine[...] + got[...]


def core_sum(mine):
    return pl.pallas_call(
        core_kernel,
        in_specs=[VMEM],
        out_specs=VMEM,
        out_shape=jax.ShapeDtypeStruct(mine.shape, F32),
        scratch_shapes=[pltpu.VMEM(mine.shape, F32), DMA, DMA],
        compiler_params=params(4),
    )(mine)


def masked_scores(k, q_block, seg_col, seg_row, start, keys):
    scores = nn(k[:keys], q_block)
    key_pos = lax.broadcasted_iota(jnp.int32, scores.shape, 0)
    query_pos = lax.broadcasted_iota(jnp.int32, scores.shape, 1) + start
    allowed = (key_pos <= query_pos) & (seg_col[:keys] == seg_row[:, start : start + QB])
    return jnp.where(allowed, scores, -1e30)


def unit_place():
    return lax.axis_index("y") * 2 + lax.axis_index("core")


def unit_device(place):
    return {"y": place // 2, "core": place % 2}


def head_swap(send, units, sems, rsems):
    iy = lax.axis_index("y")

    def copy(slot, step, owner):
        return remote(
            send.at[(iy + step) % 4, slot],
            units.at[slot, :, :, rows_of(owner * 256)],
            sems.at[slot, step - 1],
            rsems.at[slot, step - 1],
            {"y": (iy + step) % 4},
        )

    def begin(slot):
        for step in range(1, 4):
            if slot < 2:
                copy(slot, step, iy).start()
            else:
                pl.when(((iy + step) % 4 == 0) & (lax.axis_index("core") == 0))(
                    lambda step=step: copy(2, step, iy).start()
                )

    def arrive(slot):
        units[slot, :, :, rows_of(iy * 256)] = send[iy, slot]
        for step in range(1, 4):
            copy(slot, step, (iy + 4 - step) % 4).wait_recv()

    def sent():
        for slot in range(2):
            for step in range(1, 4):
                copy(slot, step, iy).wait_send()
        for step in range(1, 4):
            pl.when(((iy + step) % 4 == 0) & (lax.axis_index("core") == 0))(
                lambda step=step: copy(2, step, iy).wait_send()
            )

    return begin, arrive, sent


def result_swap(units, got, sems, rsems):
    iy, core = lax.axis_index("y"), lax.axis_index("core")

    def copy(slot, step, owner):
        to = (iy + step) % 4
        return remote(
            units.at[slot, :, :, rows_of(to * 256)],
            got.at[owner, core, slot],
            sems.at[slot, step - 1],
            rsems.at[slot, step - 1],
            {"y": to},
        )

    def hand_on(slot, which):
        part = got.at[:, which, slot] if slot < 2 else got.at[pl.ds(0, 1), 0, 2]
        return remote(part, part, sems.at[slot, 3], rsems.at[slot, 3], {"core": 1 - core})

    def begin(slot):
        got[iy, core, slot] = units[slot, :, :, rows_of(iy * 256)]
        for step in range(1, 4):
            copy(slot, step, iy).start()

    def pass_on():
        for slot in range(2):
            for step in range(1, 4):
                copy(slot, step, (iy + 4 - step) % 4).wait_recv()
            hand_on(slot, core).start()

        @pl.when(core == 0)
        def _():
            for step in range(1, 4):
                pl.when(iy == step)(lambda step=step: copy(2, step, 0).wait_recv())
            hand_on(2, 0).start()

    def finish(count):
        for slot in range(2):
            hand_on(slot, 1 - core).wait_recv()
            hand_on(slot, core).wait_send()
        pl.when(core == 1)(lambda: hand_on(2, 0).wait_recv())
        pl.when(core == 0)(lambda: hand_on(2, 0).wait_send())

        def ends(slot, _):
            for step in range(1, 4):
                copy(slot, step, iy).wait_send()
            return 0

        lax.fori_loop(0, count, ends, 0)

    return begin, pass_on, finish


def front_kernel(
    x_src,
    g_src,
    block,
    down_block,
    seg_row_ref,
    seg_col_ref,
    qkv_w,
    out_w,
    up_w,
    down_w,
    g_ref,
    normed1_ref,
    standard1_ref,
    inv_std1_ref,
    qkv_ref,
    out_ref,
    lse_ref,
    attn_ref,
    resid_ref,
    normed2_ref,
    standard2_ref,
    inv_std2_ref,
    vector_ref,
    z_blocks,
    blocks,
    x_got,
    g_got,
    quad,
    quads,
    vector_quad,
    natural,
    x_ref,
    slabs_q,
    slabs_o,
    send,
    got,
    xsend,
    xrecv,
    gsend,
    grecv,
    zsend,
    zrecv,
    core_send,
    core_recv,
    local,
    *sems,
):
    me = greet_col()
    ix, iy, core, iz = (lax.axis_index(a) for a in ("x", "y", "core", "row"))
    for step in (1, -1):
        signal(ring("row", step))
    pl.semaphore_wait(pltpu.get_barrier_semaphore(), 33)
    groups = ((0, ATTN_ROWS), (ATTN_ROWS, FF_ROWS))

    d_begin, d_middle, d_finish, d_end, _ = ring_gather(
        DOWN_FLOWS, (down_block,), lambda slab, x, y, rows, z: down_w.at[z, x, y, rows], sems[8], sems[9], 3
    )

    def zcopy(group, kind, owner):
        first, count = groups[group]
        cut = count // 32 * 16
        part = (pl.ds(first, count), pl.ds(first, cut), pl.ds(first + cut, count - cut))[max(kind - 1, 0)]
        return remote(
            block.at[part] if kind < 2 else z_blocks.at[owner, part],
            z_blocks.at[owner, part],
            zsend.at[group, kind],
            zrecv.at[group, kind],
            ring("row", 1 if kind % 2 == 0 else -1),
        )

    for group in range(2):
        for kind in (0, 1):
            zcopy(group, kind, iz).start()
    x_begin, x_end = token_swap(x_src, x_got, xsend, xrecv, local.at[0], me)
    g_begin, g_end = token_swap(g_src, g_got, gsend, grecv, local.at[1], me)
    d_begin(0)
    own = pltpu.make_async_copy(down_block, down_w.at[iz, ix, iy], local.at[2])
    own.start()
    z_blocks[iz] = block[...]
    d_middle(0)
    d_finish(0)
    own.wait()
    d_begin(1)
    x_begin()
    for group in range(2):
        for kind in (0, 1):
            near = (iz + (3 if kind == 0 else 1)) % 4
            zcopy(group, kind, near).wait_recv()
            zcopy(group, kind + 2, near).start()

    def join(group):
        first, count = groups[group]
        for kind in (2, 3):
            zcopy(group, kind, (iz + 2) % 4).wait_recv()
        total = None
        for owner in range(4):
            shape = (block.shape[1], blocks.shape[1])
            row = lax.broadcasted_iota(jnp.int32, shape, 0) + owner * shape[0]
            place = (row == lax.broadcasted_iota(jnp.int32, shape, 1)).astype(F32).astype(BF16)
            part = nn(z_blocks[owner, first : first + count], place)
            total = part if total is None else total + part
        blocks[first : first + count] = total.astype(BF16)

    attn_blocks = (blocks.at[pl.ds(0, QKV_ROWS)], blocks.at[pl.ds(QKV_ROWS, OUT_ROWS)])
    up_block = blocks.at[pl.ds(ATTN_ROWS, FF_ROWS)]
    a_begin, a_middle, a_finish, a_end, a_at = ring_gather(
        ATTN_FLOWS,
        attn_blocks,
        lambda slab, x, y, rows, z: (slabs_q, slabs_o)[slab].at[x, y, core, rows],
        sems[0],
        sems[1],
    )
    f_begin, f_middle, f_finish, f_end, _ = ring_gather(
        UP_FLOWS, (up_block,), lambda slab, x, y, rows, z: up_w.at[x, y, rows], sems[2], sems[3]
    )
    swaps = []

    def swap(flow, part, owner):
        slab, first, count, _, _ = ATTN_FLOWS[flow]
        rows = pl.ds(first, count)
        every = pl.ds(0, 4)
        by_x = "xy"[(ATTN_FLOWS[flow][4] + 1) % 2] == "x"

        def view(which):
            ref = (slabs_q, slabs_o)[slab]
            return ref.at[owner if by_x else every, every if by_x else owner, which, rows]

        def copy(which):
            return remote(
                view(which), view(which), core_send.at[flow, part], core_recv.at[flow, part], {"core": 1 - core}
            )

        copy(core).start()
        swaps.append((copy(core), copy(1 - core)))

    join(0)
    slabs_q[ix, iy, core] = blocks[:QKV_ROWS]
    slabs_o[ix, iy, core] = blocks[QKV_ROWS:ATTN_ROWS]
    a_begin(0)
    join(1)
    f_begin(0)
    own_up = pltpu.make_async_copy(up_block, up_w.at[ix, iy], local.at[3])
    own_up.start()
    a_middle(0)
    a_finish(0)
    a_begin(1)
    for flow in range(len(ATTN_FLOWS)):
        swap(flow, 0, a_at(flow, 1, 0))
    d_middle(1)
    d_finish(1)
    d_begin(2)
    f_middle(0)
    f_finish(0)
    own_up.wait()

    x_end()
    lay_out(lambda device: x_got[device, :34].astype(F32), quad, x_ref)
    eye_shape = (48, 128)
    eye = lax.broadcasted_iota(jnp.int32, eye_shape, 0) == lax.broadcasted_iota(jnp.int32, eye_shape, 1)
    eye = eye.astype(F32).astype(BF16)

    def vectors(device):
        rows = x_got[device, 32:48, :128]
        turned = nt(eye, rows)
        return turned[:34]

    lay_out(vectors, vector_quad, vector_ref)

    def vector(i):
        return vector_ref[:, 2 + i : 3 + i]

    normed1, standard1, inv_std1 = norm_in(x_ref[...], vector(3), vector(4))
    full = x_ref.shape[0]
    extra = normed1_ref.shape[0] - full
    ones_row = (lax.broadcasted_iota(jnp.int32, (extra, 256), 0) == 0).astype(F32).astype(BF16)
    normed1_ref[:full] = normed1
    normed1_ref[full:] = ones_row
    standard1_ref[...] = standard1
    inv_std1_ref[...] = inv_std1

    a_middle(1, swap)
    f_begin(1)
    g_begin()
    a_finish(1, swap)
    for out, come in swaps:
        come.wait_recv()

    keep = [
        pltpu.make_async_copy(slabs_q, qkv_w, local.at[4]),
        pltpu.make_async_copy(slabs_o, out_w, local.at[5]),
    ]
    for c in keep:
        c.start()

    def project(step, _):
        w = slabs_q[step // 2, pl.ds(step % 2 * 2, 2)]
        quads[...] = nn(w.reshape(4 * QKV_ROWS, full), normed1_ref[:full])
        rows = pl.ds(pl.multiple_of(step * 136, 8), 136)
        for j in range(3):
            for part in range(4):
                quad[34 * part : 34 * part + 34] = quads[112 * part + 34 * j : 112 * part + 34 * j + 34]
            value = quad[...]
            if j != 1:
                value = value + vector_ref[rows, 2 + j // 2 : 3 + j // 2]
            natural[j, rows] = value
        return 0

    lax.fori_loop(0, 8, project, 0)
    count = jnp.where(unit_place() == 0, 3, 2)
    begin, arrive, sent = head_swap(send, qkv_ref, sems[4], sems[5])
    begin_result, pass_on, finish = result_swap(out_ref, got, sems[6], sems[7])
    for slot in range(3):

        def heads(y, _, slot=slot):
            head = slot * 8 + y * 2 + core if slot < 2 else HEADS - 1
            start = head * HD if slot == 2 else pl.multiple_of(head * HD, HD)
            for j in range(3):
                send[y, slot, j] = natural[j, pl.ds(start, HD)].astype(BF16)
            return 0

        lax.fori_loop(0, 4, heads, 0)
        begin(slot)

    def unit(slot, _):
        arrive(slot)
        q = qkv_ref[slot, 0] * (HD**-0.5)
        k = qkv_ref[slot, 1].T
        v = qkv_ref[slot, 2]
        for start in range(0, q.shape[1], QB):
            keys = start + QB
            scores = masked_scores(
                k, q[:, start:keys], seg_col_ref[...], seg_row_ref[...], start, keys
            )
            top = jnp.max(scores, 0, keepdims=True)
            weights = jnp.exp(scores - top)
            total = jnp.sum(weights, 0, keepdims=True)
            result = nn(v[:, :keys], weights.astype(BF16)) * (1.0 / total)
            out_ref[slot, 0, :, start:keys] = result.astype(BF16)
            lse_ref[slot, :, start:keys] = top + jnp.log(total)
        begin_result(slot)
        return 0

    d_middle(2)
    lax.fori_loop(0, count, unit, 0)
    f_middle(1)
    sent()
    pass_on()
    finish(count)

    for head in range(HEADS):
        owner = head % 8
        attn_ref[head * HD : head * HD + HD] = got[owner // 2, owner % 2, head // 8, 0]

    def project_out(step, _):
        w = slabs_o[step // 2, pl.ds(step % 2 * 2, 2)]
        result = nn(w.reshape(4 * OUT_ROWS, full), attn_ref[...])
        quads[: 4 * OUT_ROWS] = result
        rows = pl.ds(pl.multiple_of(step * 136, 8), 136)
        for part in range(4):
            quad[34 * part : 34 * part + 34] = quads[48 * part : 48 * part + 34]
        resid_ref[rows] = x_ref[rows] + quad[...] + vector_ref[rows, 4:5]
        return 0

    lax.fori_loop(0, 8, project_out, 0)
    normed2, standard2, inv_std2 = norm_in(resid_ref[...], vector(5), vector(6))
    normed2_ref[...] = normed2
    standard2_ref[...] = standard2
    inv_std2_ref[...] = inv_std2
    g_end()
    lay_out(lambda device: g_got[device, :34].astype(F32), quad, natural.at[0])
    g_ref[...] = natural[0].astype(BF16)

    f_finish(1)
    d_finish(2)
    a_end()
    f_end()
    d_end()
    for group in range(2):
        for kind in range(4):
            zcopy(group, kind, iz).wait_send()
    for out, _ in swaps:
        out.wait_send()
    for c in keep:
        c.wait()


def front(x_src, g_src, block, down_block, seg_row, seg_col):
    length = seg_row.shape[1]
    full = 4 * block.shape[1]
    total = block.shape[0]
    flat = jax.ShapeDtypeStruct((full, 256), F32)
    low = jax.ShapeDtypeStruct((full, 256), BF16)
    stat = jax.ShapeDtypeStruct((1, 256), F32)
    return pl.pallas_call(
        front_kernel,
        in_specs=[ANY, ANY, VMEM, ANY, VMEM, VMEM],
        out_specs=[ANY] * 4 + [VMEM] * 13,
        out_shape=[
            jax.ShapeDtypeStruct((4, 4, 2, QKV_ROWS, full), BF16),
            jax.ShapeDtypeStruct((4, 4, 2, OUT_ROWS, full), BF16),
            jax.ShapeDtypeStruct((4, 4, FF_ROWS, full), BF16),
            jax.ShapeDtypeStruct((4, 4, 4, DOWN_ROWS, DOWN_MAIN), BF16),
            low,
            jax.ShapeDtypeStruct((WIDE, 256), BF16),
            flat,
            stat,
            jax.ShapeDtypeStruct((3, 3, HD, length), BF16),
            jax.ShapeDtypeStruct((3, 1, HD, length), BF16),
            jax.ShapeDtypeStruct((3, 1, length), F32),
            low,
            flat,
            low,
            flat,
            stat,
            jax.ShapeDtypeStruct((full, 16), F32),
        ],
        scratch_shapes=[
            pltpu.VMEM((4, total, block.shape[1]), BF16),
            pltpu.VMEM((total, full), BF16),
            pltpu.VMEM((32, 48, 256), BF16),
            pltpu.VMEM((32, 48, 256), BF16),
            pltpu.VMEM((136, 256), F32),
            pltpu.VMEM((4 * QKV_ROWS, 256), F32),
            pltpu.VMEM((136, 16), F32),
            pltpu.VMEM((3, full, 256), F32),
            pltpu.VMEM((full, 256), F32),
            pltpu.VMEM((4, 4, 2, QKV_ROWS, full), BF16),
            pltpu.VMEM((4, 4, 2, OUT_ROWS, full), BF16),
            pltpu.VMEM((4, 3, 3, HD, 256), BF16),
            pltpu.VMEM((4, 2, 3, 1, HD, 256), BF16),
            DMA((32,)),
            DMA((32,)),
            DMA((32,)),
            DMA((32,)),
            DMA((2, 4)),
            DMA((2, 4)),
            DMA((3, 4)),
            DMA((3, 4)),
            DMA((6,)),
            DMA((3, 2, 4)),
            DMA((3, 2, 4)),
            DMA((2, 2, 4)),
            DMA((2, 2, 4)),
            DMA((3, 3)),
            DMA((3, 3)),
            DMA((3, 4)),
            DMA((3, 4)),
            DMA((1, 3, 4)),
            DMA((1, 3, 4)),
        ],
        compiler_params=params(0, 60),
    )(x_src, g_src, block, down_block, seg_row, seg_col)


def regroup(step, source, target):
    quad = source[pl.ds(pl.multiple_of(step * 136, 8), 136)]
    for part in range(4):
        target(part, quad[34 * part : 34 * part + 34])


def back_kernel(
    send,
    seg_row_ref,
    seg_col_ref,
    qkv_ref,
    out_ref,
    lse_ref,
    wide,
    out_in,
    up_in,
    active_ref,
    g_ref,
    qkv_w,
    normed_ref,
    standard_ref,
    inv_std_ref,
    gain_ref,
    dresid_ref,
    wide_out,
    input_out,
    main_out,
    tail_out,
    down_out,
    column_out,
    down_in,
    grad_ref,
    dqkv_ref,
    dk_ref,
    dv_ref,
    got,
    natural,
    slab_ref,
    slabs,
    w_buf,
    acc,
    columns,
    column_slab,
    column_part,
    column_sum,
    z_column,
    input_slab,
    input_slabs,
    qkv_part,
    sums,
    z_main,
    z_tail,
    wsend,
    wrecv,
    isend,
    irecv,
    zsend,
    zrecv,
    local,
    w_sem,
    *rest,
):
    place = greet_col()
    ix, iy, core, iz = (lax.axis_index(a) for a in ("x", "y", "core", "row"))
    xy = ix * 4 + iy
    for step in range(1, 4):
        signal(ring("row", step))
    pl.semaphore_wait(pltpu.get_barrier_semaphore(), 34)
    count = jnp.where(unit_place() == 0, 3, 2)
    begin, arrive, sent = head_swap(send, grad_ref, rest[0], rest[1])
    begin_result, pass_on, finish = result_swap(dqkv_ref, got, rest[2], rest[3])
    counts = (len(FIRST_FLOWS) * 8, len(LAST_FLOWS) * 8)
    bufs = rest[12:]
    sum_refs = [sums.at[:, pl.ds(at, rows)] for at, rows in zip(SUM_FIRST, SUM_ROWS)]
    first = ring_reduce(FIRST_FLOWS, (out_in, up_in), sum_refs[:2], bufs[: counts[0]], rest[4], rest[5])
    last = ring_reduce(
        LAST_FLOWS, (qkv_part,), sum_refs[2:], bufs[counts[0] : sum(counts)], rest[6], rest[7]
    )
    down = ring_reduce(
        DOWN_FLOWS, (down_in,), (down_out,), bufs[sum(counts) : sum(counts) + 12], rest[8], rest[9], True
    )
    cols = ring_reduce(
        COLUMN_FLOWS, (column_part,), (column_sum,), bufs[sum(counts) + 12 :], rest[10], rest[11]
    )
    for slot in range(3):
        begin(slot)
    first[0](0)

    tail_rows = g_ref.shape[0] // 4 - DOWN_MAIN

    def down_part(z):
        start = z * (DOWN_MAIN + tail_rows)
        main = g_ref[pl.ds(pl.multiple_of(start, 16), DOWN_MAIN)]
        tail = g_ref[pl.ds(pl.multiple_of(start + DOWN_MAIN, 16), tail_rows)]

        def one(slab, _):
            units = active_ref[slab]
            down_in[z, slab, :FF_ROWS] = nt(units, main).astype(BF16)
            turned = nt(tail, units).astype(BF16)
            down_in[z, slab, FF_ROWS:] = jnp.concatenate(
                [turned, jnp.zeros((tail_rows, DOWN_MAIN - FF_ROWS), BF16)], 1
            )
            return 0

        lax.fori_loop(0, 16, one, 0)

    down_part((iz + 2) % 4)
    down[0](0, (0, 1))
    down_part((iz + 1) % 4)
    down_part((iz + 3) % 4)
    down[0](0, (2, 3))

    def copy_wide(step, owner):
        peer = (place + step) % 32
        return remote(
            wide.at[peer], wide_out.at[owner], wsend.at[step], wrecv.at[step], col_device(peer)
        )

    def begin_wide(step, _):
        copy_wide(step, place).start()
        return 0

    lax.fori_loop(1, 32, begin_wide, 0)
    own = pltpu.make_async_copy(wide.at[place], wide_out.at[place], local)
    own.start()

    def copy_w(step):
        return pltpu.make_async_copy(
            qkv_w.at[pl.ds(step * 4, 4)], w_buf.at[step % 2], w_sem.at[step % 2]
        )

    copy_w(0).start()

    def unit(slot, _):
        arrive(slot)
        q = qkv_ref[slot, 0] * (HD**-0.5)
        key_cols = qkv_ref[slot, 1]
        k = key_cols.T
        v = qkv_ref[slot, 2].T
        grad = grad_ref[slot, 0]
        delta = jnp.sum(grad.astype(F32) * out_ref[slot, 0].astype(F32), 0, keepdims=True)
        dk_ref[...] = jnp.zeros_like(dk_ref)
        dv_ref[...] = jnp.zeros_like(dv_ref)
        for start in range(0, q.shape[1], QB):
            keys = start + QB
            scores = masked_scores(
                k, q[:, start:keys], seg_col_ref[...], seg_row_ref[...], start, keys
            )
            weights = jnp.exp(scores - lse_ref[slot, :, start:keys])
            dweights = nn(v[:keys], grad[:, start:keys])
            dscores = (weights * (dweights - delta[:, start:keys])).astype(BF16)
            dq = nn(key_cols[:, :keys], dscores) * (HD**-0.5)
            dqkv_ref[slot, 0, :, start:keys] = dq.astype(BF16)
            dk_ref[:, :keys] += nt(q[:, start:keys], dscores)
            dv_ref[:, :keys] += nt(grad[:, start:keys], weights.astype(BF16))
        dqkv_ref[slot, 1] = dk_ref[...].astype(BF16)
        dqkv_ref[slot, 2] = dv_ref[...].astype(BF16)
        begin_result(slot)
        return 0

    lax.fori_loop(0, count, unit, 0)
    first[1](0)
    down[1](0)
    down_part(iz)
    sent()
    pass_on()
    finish(count)

    for head in range(HEADS):
        owner = head % 8
        for j in range(3):
            natural[j, head * HD : head * HD + HD] = got[owner // 2, owner % 2, head // 8, j].astype(F32)
    slab_ref[...] = jnp.zeros_like(slab_ref)
    acc[...] = jnp.zeros_like(acc)

    def by_slab(step, _):
        for j in range(3):

            def put(part, rows, j=j):
                slab_ref[part, 34 * j : 34 * j + 34] = rows

            regroup(step, natural.at[j], put)
        four = slab_ref[...].astype(BF16)
        slabs[pl.ds(step * 4, 4)] = four
        return 0

    lax.fori_loop(0, 8, by_slab, 0)

    def weight_part(step, _):
        index = step * 2 + core
        part = nt(slabs[index], normed_ref[...])
        qkv_part[step // 4, step % 4] = part.astype(BF16)
        return 0

    lax.fori_loop(0, 16, weight_part, 0)
    last[0](0)

    def product(step, _):
        @pl.when(step < 7)
        def _():
            copy_w(step + 1).start()

        copy_w(step).wait()
        acc[...] += lax.dot_general(
            slabs[pl.ds(step * 4, 4)].reshape(4 * QKV_ROWS, 256),
            w_buf[step % 2].reshape(4 * QKV_ROWS, -1),
            (((0,), (0,)), ((), ())),
            preferred_element_type=F32,
        )
        return 0

    lax.fori_loop(0, 8, product, 0)
    first[2](0)
    first[0](1)

    late = [
        pltpu.make_async_copy(standard_ref, natural.at[1], w_sem.at[0]),
        pltpu.make_async_copy(dresid_ref, natural.at[2], w_sem.at[1]),
    ]
    for c in late:
        c.start()
    dnormed = acc[...].T
    for c in late:
        c.wait()
    standard = natural[1]
    dv = dnormed * gain_ref[...]
    back = inv_std_ref[...] * (
        dv - jnp.mean(dv, 0, keepdims=True) - standard * jnp.mean(dv * standard, 0, keepdims=True)
    )
    natural[0] = natural[2] + back
    lane = lax.broadcasted_iota(jnp.int32, columns.shape, 1)
    gain_col = jnp.sum(dnormed * standard, 1, keepdims=True)
    shift_col = jnp.sum(dnormed, 1, keepdims=True)
    columns[...] = jnp.where(lane == 65, gain_col, jnp.where(lane == 66, shift_col, 0.0))
    input_slab[...] = jnp.zeros_like(input_slab)
    column_slab[...] = jnp.zeros_like(column_slab)

    def spread(step, _):
        def put(part, rows):
            input_slab[part, :34] = rows

        def put_column(part, rows):
            column_slab[step * 4 + part, :34] = rows

        regroup(step, natural.at[0], put)
        regroup(step, columns, put_column)
        input_slabs[pl.ds(step * 4, 4)] = input_slab[...].astype(BF16)
        return 0

    lax.fori_loop(0, 8, spread, 0)

    def copy_input(step, owner):
        peer = (xy + step) % 16
        return remote(
            input_slabs.at[peer * 2 + core],
            input_out.at[owner],
            isend.at[step],
            irecv.at[step],
            {"x": peer // 4, "y": peer % 4},
        )

    def own_columns(step, _):
        column_part[step // 4, step % 4] = column_slab[step * 2 + core].astype(BF16)
        return 0

    lax.fori_loop(0, 16, own_columns, 0)
    cols[0](0)
    down[2](0)
    down[0](1)

    def begin_input(step, _):
        copy_input(step, xy).start()
        return 0

    lax.fori_loop(1, 16, begin_input, 0)
    input_out[xy] = input_slabs[xy * 2 + core]

    def z_columns(step):
        return remote(
            column_sum, z_column.at[pl.ds(step - 1, 1)], zsend.at[2, 0, step - 1], zrecv.at[2, 0, step - 1], ring("row", step)
        )

    def z_copies(group, step):
        rows = pl.ds(0, SUM_FIRST[2]) if group == 0 else pl.ds(SUM_FIRST[2], QKV_ROWS)
        window = pl.ds(pl.multiple_of((iz + step) % 4 * 256, 256), WINDOW)
        return [
            remote(
                sums.at[0, rows, lanes],
                out.at[step - 1, rows],
                zsend.at[group, i, step - 1],
                zrecv.at[group, i, step - 1],
                ring("row", step),
            )
            for i, (lanes, out) in enumerate(((window, z_main), (pl.ds(WIDE - LANE, LANE), z_tail)))
        ]

    def begin_z(group):
        for step in range(1, 4):
            for c in z_copies(group, step):
                c.start()

    first[1](1)
    down[1](1)
    last[1](0)
    first[2](1)
    begin_z(0)
    cols[1](0)
    last[2](0)
    last[0](1)
    cols[2](0)
    cols[0](1)
    down[2](1)
    down[0](2)
    last[1](1)
    cols[1](1)
    down[1](2)
    last[2](1)
    begin_z(1)
    cols[2](1)
    for step in range(1, 4):
        z_columns(step).start()
    down[2](2)
    first[3]()
    last[3]()
    down[3]()
    cols[3]()
    own.wait()

    def end_wide(step, _):
        copy_wide(step, (place + 32 - step) % 32).wait()
        return 0

    lax.fori_loop(1, 32, end_wide, 0)

    def end_input(step, _):
        copy_input(step, (xy + 16 - step) % 16).wait()
        return 0

    lax.fori_loop(1, 16, end_input, 0)
    for group in range(2):
        for step in range(1, 4):
            for c in z_copies(group, step):
                c.wait()
    for step in range(1, 4):
        z_columns(step).wait()
    column_out[...] = column_sum[0].astype(F32) + sum(z_column[i].astype(F32) for i in range(3))
    window = pl.ds(pl.multiple_of(iz * 256, 256), WINDOW)
    main_out[...] = sums[0, :, window].astype(F32) + sum(z_main[i].astype(F32) for i in range(3))
    tail_out[...] = sums[0, :, WIDE - LANE :].astype(F32) + sum(z_tail[i].astype(F32) for i in range(3))


def attend_back(
    send, seg_row, seg_col, qkv, out, lse, wide, out_part, up_part, active, g, qkv_w, normed, standard, inv_std, gain, dresid
):
    length = seg_row.shape[1]
    full = qkv_w.shape[-1]
    first_sems, first_bufs = ring_bufs(FIRST_FLOWS, WIDE)
    last_sems, last_bufs = ring_bufs(LAST_FLOWS, WIDE)
    down_sems, down_bufs = ring_bufs(DOWN_FLOWS, DOWN_MAIN, True)
    column_sems, column_bufs = ring_bufs(COLUMN_FLOWS, LANE)
    total = sum(SUM_ROWS)
    return pl.pallas_call(
        back_kernel,
        in_specs=[VMEM] * 6 + [ANY] + [VMEM] * 4 + [ANY, VMEM, ANY, VMEM, VMEM, ANY],
        out_specs=[ANY] + [VMEM] * 5,
        out_shape=[
            jax.ShapeDtypeStruct(wide.shape, wide.dtype),
            jax.ShapeDtypeStruct((16, 48, 256), BF16),
            jax.ShapeDtypeStruct((total, WINDOW), F32),
            jax.ShapeDtypeStruct((total, LANE), F32),
            jax.ShapeDtypeStruct((1, DOWN_ROWS, DOWN_MAIN), F32),
            jax.ShapeDtypeStruct((48, LANE), F32),
        ],
        scratch_shapes=[
            pltpu.VMEM((4, 16, DOWN_ROWS, DOWN_MAIN), BF16),
            pltpu.VMEM((3, 1, HD, length), BF16),
            pltpu.VMEM((3, 3, HD, length), BF16),
            pltpu.VMEM((HD, length), F32),
            pltpu.VMEM((HD, length), F32),
            pltpu.VMEM((4, 2, 3, 3, HD, 256), BF16),
            pltpu.VMEM((3, full, 256), F32),
            pltpu.VMEM((4, QKV_ROWS, 256), F32),
            pltpu.VMEM((32, QKV_ROWS, 256), BF16),
            pltpu.VMEM((2, 4, QKV_ROWS, full), BF16),
            pltpu.VMEM((256, full), F32),
            pltpu.VMEM((full, LANE), F32),
            pltpu.VMEM((32, 48, LANE), F32),
            pltpu.VMEM((4, 4, 48, LANE), BF16),
            pltpu.VMEM((1, 48, LANE), BF16),
            pltpu.VMEM((3, 48, LANE), BF16),
            pltpu.VMEM((4, 48, 256), F32),
            pltpu.VMEM((32, 48, 256), BF16),
            pltpu.VMEM((4, 4, QKV_ROWS, WIDE), BF16),
            pltpu.VMEM((1, total, WIDE), BF16),
            pltpu.VMEM((3, total, WINDOW), BF16),
            pltpu.VMEM((3, total, LANE), BF16),
            DMA((32,)),
            DMA((32,)),
            DMA((16,)),
            DMA((16,)),
            DMA((3, 2, 3)),
            DMA((3, 2, 3)),
            DMA,
            DMA((2,)),
            DMA((3, 3)),
            DMA((3, 3)),
            DMA((3, 4)),
            DMA((3, 4)),
        ]
        + first_sems
        + last_sems
        + down_sems
        + column_sems
        + first_bufs
        + last_bufs
        + down_bufs
        + column_bufs,
        compiler_params=params(6, 62),
    )(
        send, seg_row, seg_col, qkv, out, lse, wide, out_part, up_part, active, g, qkv_w, normed, standard, inv_std, gain, dresid
    )


def norm_back(dn, standard, inv_std, gain):
    dv = dn * gain
    back = inv_std * (
        dv - jnp.mean(dv, 0, keepdims=True) - standard * jnp.mean(dv * standard, 0, keepdims=True)
    )
    return back, jnp.sum(dn * standard, 1), jnp.sum(dn, 1)


def to_heads(v, core):
    n, _, tokens = v.shape
    heads = v.reshape(n, HEADS, HD, tokens).transpose(1, 0, 2, 3)
    pairs = heads[:16].reshape(2, 4, 2, n, HD, tokens)
    mine = lax.dynamic_index_in_dim(pairs, core, 2, keepdims=False)
    last = jnp.broadcast_to(heads[16:], (4, n, HD, tokens))
    return jnp.concatenate([mine.transpose(1, 0, 2, 3, 4), last[:, None]], 1)


def shards(
    layer_input,
    cotangent,
    segments,
    qkv_weight,
    qv_bias,
    out_weight,
    out_bias,
    up_weight,
    up_bias,
    down_weight,
    down_bias,
    first_gain,
    first_shift,
    second_gain,
    second_shift,
):
    ix, iy, core = lax.axis_index("x"), lax.axis_index("y"), lax.axis_index("core")
    width = layer_input.shape[0]
    rows = qkv_weight.shape[0]
    full = 4 * rows
    units = up_weight.shape[1]

    block = jnp.concatenate(
        [
            qkv_weight.transpose(1, 2, 0).reshape(3 * width, rows),
            jnp.pad(up_bias[None], ((0, QKV_ROWS - 3 * width - 1), (0, rows - units))),
            jnp.pad(out_weight.T, ((0, OUT_ROWS - width), (0, 0))),
            jnp.pad(up_weight.T, ((0, FF_ROWS - units), (0, 0))),
        ],
        0,
    )
    down_block = jnp.concatenate(
        [
            jnp.pad(down_weight[:, :DOWN_MAIN], ((0, FF_ROWS - units), (0, 0))),
            jnp.pad(down_weight[:, DOWN_MAIN:].T, ((0, 0), (0, DOWN_MAIN - units))),
        ],
        0,
    )
    small = jnp.concatenate(
        [qv_bias, jnp.stack([out_bias, first_gain, first_shift, second_gain, second_shift])], 0
    )
    small = jnp.tile(jnp.pad(small, ((0, 48 - width - 7), (0, 256 - width))), (1, 16))
    x_src = jnp.concatenate([layer_input, small], 0)
    g_src = jnp.pad(cotangent, ((0, 48 - width), (0, 0)))
    seg = lax.dynamic_index_in_dim(segments, ix, 0, keepdims=False)
    seg_row, seg_col = seg[None], seg[:, None]
    (
        qkv_w,
        out_w,
        up_w,
        down_w,
        g_low,
        normed1,
        standard1,
        inv_std1,
        units_qkv,
        units_out,
        lse,
        attn,
        resid,
        normed2,
        standard2,
        inv_std2,
        vectors,
    ) = front(x_src, g_src, block, down_block, seg_row, seg_col)
    qkv_w = qkv_w.reshape(32, QKV_ROWS, full)
    out_w = out_w.reshape(32, OUT_ROWS, full)
    up_w = up_w.reshape(16, FF_ROWS, full)
    down_w = down_w.reshape(4, 16, DOWN_ROWS, DOWN_MAIN)
    down_tail = down_w[:, :, FF_ROWS:, :FF_ROWS]
    g = g_low.astype(F32)
    gain1, gain2 = vectors[:, 5:6], vectors[:, 7:8]
    hidden_bias = lax.dynamic_index_in_dim(
        qkv_w[:, 3 * width, :units].reshape(16, 2, units), core, 1, keepdims=False
    ).astype(F32)
    hidden_bias = jnp.pad(hidden_bias, ((0, 0), (0, FF_ROWS - units)))
    hidden = jnp.einsum("xfd,dt->xft", up_w, normed2, preferred_element_type=F32) + hidden_bias[..., None]
    active, gelu_back = jax.vjp(lambda h: jax.nn.gelu(h, approximate=True), hidden)
    active = active.astype(BF16)
    active_rows = jnp.pad(active, ((0, 0), (0, DOWN_ROWS - FF_ROWS), (0, 0)))
    out_main = [
        jnp.einsum("xfd,xft->dt", down_w[z], active_rows, preferred_element_type=F32) for z in range(4)
    ]
    out_tail = jnp.einsum("zxdf,xft->zdt", down_tail, active, preferred_element_type=F32)
    ff_out = jnp.concatenate([p for z in range(4) for p in (out_main[z], out_tail[z])], 0)
    send_out = (ff_out + jnp.where(core == 0, 1.0, 0.0) * resid).astype(BF16)
    send_out = jnp.pad(send_out.reshape(32, width, 256), ((0, 0), (0, 48 - width), (0, 0)))
    g_main = [g_low[z * rows : z * rows + DOWN_MAIN] for z in range(4)]
    g_tail = jnp.stack([g_low[z * rows + DOWN_MAIN : z * rows + rows] for z in range(4)])
    dactive = sum(
        jnp.einsum("xfd,dt->xft", down_w[z], g_main[z], preferred_element_type=F32) for z in range(4)
    )[:, :FF_ROWS]
    dactive = dactive + jnp.einsum("zxdf,zdt->xft", down_tail, g_tail, preferred_element_type=F32)
    dhidden = gelu_back(dactive)[0].astype(BF16)
    extra = WIDE - full
    ones_row = jnp.pad(jnp.ones((1, 256), BF16), ((0, extra - 1), (0, 0)))

    def widen(v):
        return jnp.concatenate([v, ones_row], 0)

    up_part = jnp.einsum("xft,dt->xfd", dhidden, widen(normed2), preferred_element_type=F32).astype(BF16)
    dn2 = jnp.einsum("xfd,xft->dt", up_w, dhidden, preferred_element_type=F32)
    dn2 = core_sum(dn2)
    back2, gain2_grad, shift2_grad = norm_back(dn2, standard2, inv_std2, gain2)
    dresid = g + back2
    dproj = dresid.astype(BF16)
    dproj_block = jnp.pad(dproj.reshape(32, width, 256), ((0, 0), (0, OUT_ROWS - width), (0, 0)))
    dattn = jnp.einsum("ced,cet->dt", out_w, dproj_block, preferred_element_type=F32).astype(BF16)
    mine = lax.dynamic_index_in_dim(dproj_block.reshape(16, 2, OUT_ROWS, 256), core, 1, keepdims=False)
    cols = jnp.stack([jnp.sum(g, -1), gain2_grad, shift2_grad], -1).reshape(16, 2, width, 3)
    cols = lax.dynamic_index_in_dim(cols, core, 1, keepdims=False)
    cols = jnp.pad(cols, ((0, 0), (0, OUT_ROWS - width), (full + 1, extra - 4)))
    out_part = jnp.einsum("xrt,dt->xrd", mine, widen(attn), preferred_element_type=F32) + cols
    got_out, input_got, main, tail, down_sum, columns = attend_back(
        to_heads(dattn[None], core),
        seg_row,
        seg_col,
        units_qkv,
        units_out,
        lse,
        send_out,
        out_part.astype(BF16).reshape(4, 4, OUT_ROWS, WIDE),
        up_part.reshape(4, 4, FF_ROWS, WIDE),
        active,
        g_low,
        qkv_w,
        normed1,
        standard1,
        inv_std1,
        gain1,
        dresid,
    )
    layer_output = jnp.sum(got_out[:, :width].reshape(16, 2, width, 256).astype(F32), 1)
    layer_output = layer_output.transpose(1, 0, 2).reshape(width, 4096)
    layer_output = layer_output + down_bias.astype(F32)[:, None]
    input_grad = input_got[:, :width].transpose(1, 0, 2).reshape(width, 4096).astype(F32)
    main = lax.dynamic_slice_in_dim(main, lax.axis_index("row") * (rows - 256), rows, 1)
    out_first, up_first, qkv_first = SUM_FIRST
    qkv_out = main[qkv_first : qkv_first + 3 * width].reshape(3, width, rows).transpose(2, 0, 1)
    qkv_tail = tail[qkv_first:, LANE - extra :]
    out_tail = tail[out_first : out_first + width, LANE - extra :]
    return (
        layer_output,
        input_grad,
        qkv_out,
        jnp.stack([qkv_tail[:width, 0], qkv_tail[2 * width : 3 * width, 0]]),
        main[out_first : out_first + width].T,
        out_tail[:, 0],
        main[up_first : up_first + units].T,
        tail[up_first : up_first + units, LANE - extra],
        jnp.concatenate([down_sum[0, :units], down_sum[0, FF_ROWS:, :units].T], 1),
        out_tail[:, 1],
        columns[:width, 65],
        columns[:width, 66],
        out_tail[:, 2],
        out_tail[:, 3],
    )


def solution(mesh):
    split = Mesh(mesh.devices.reshape(4, 4, 4, 2), ("row", "x", "y", "core"))
    vec = P(COL)
    return jax.shard_map(
        shards,
        mesh=split,
        in_specs=(
            P(COL, "row"),
            P(COL, "row"),
            P("row", None),
            P("row", None, COL),
            P(None, COL),
            P("row", COL),
            vec,
            P("row", COL),
            vec,
            P(COL, "row"),
            vec,
            vec,
            vec,
            vec,
            vec,
        ),
        out_specs=(
            P(COL, "row"),
            P(COL, "row"),
            P("row", None, COL),
            P(None, COL),
            P("row", COL),
            vec,
            P("row", COL),
            vec,
            P(COL, "row"),
            vec,
            vec,
            vec,
            vec,
            vec,
        ),
        check_vma=False,
    )
```

profile of v0, /device:TPU:0, one launch (start us, length us, event | category | flops | bytes accessed | tf_op | source)
XLA Modules:
  0.0 314.1 jit_solution(3075454551173811672)
XLA Ops:
  0.7 0.7 convert_element_type.82
  1.4 0.7 broadcast_in_dim.4
  2.1 0.8 concatenate.28
  2.9 0.7 pad.80.clone
  3.6 0.6 constant_dynamic-slice_fusion.2.seg_row_ref
  4.2 0.8 slice.142
  5.1 0.9 slice.141
  6.0 0.6 fusion.55.down_block
  6.6 0.9 reshape.111
  7.6 0.7 fusion.39.block
  8.3 0.8 pad_maximum_fusion.x_src
  9.2 0.8 pad.57.g_src
  9.9 1.0 copy.52.seg_col_ref
  11.0 122.9 %shard_map.254 = (bf16[4,4,2,112,1088]{4,3,2,1,0:T(8,128)(2,1)}, bf16[4,4,2,48,1088]{4,3,2,1,0:T(8,128)(2,1)}, bf16[4,4,144,1088]{3,2,1,0:T(8,128)(2,1)}, bf16[4...) custom-call(bf16[48,4096]{1,0:T(8,128)(2,1)} %pad_maximum_fusion.x_s, ...), custom_call_target="tpu_custom_call" | custom-call | tf_op jit(solution)/shard_map/pallas_call | solution.py:735
  133.9 1.1 slice_reduce_fusion.2
  135.0 0.8 slice_bitcast_fusion.9
  135.8 2.5 fusion.77
  138.3 4.3 %multiply_convert_fusion = (bf16[16,144,256]{2,1,0:T(8,128)(2,1)S(1)}, f32[16,144,256]{2,1,0:T(8,128)S(1)}) fusion(f32[16,144]{1,0:T(8,128)S(1)} %pad_convert_fusion, bf16[16,144,1088]{2,1,0:T(8,128)(2,1)} %bitcast.210, bf16[1088,256]{1,0:T(8,128)(2,1)S(1)} %copy-done.9), kind=kOutput, calls=%fused_computation.19 | convolution fusion | flops 1289355264 | bytes 9118720 | tf_op jit(solution)/shard_map/xfd,dt->xft/dot_general | solution.py:1313
  142.6 0.4 fusion.16
  143.0 0.5 fusion.76
  143.5 0.5 fusion.15
  144.0 0.6 fusion.14
  144.6 0.6 fusion.13
  145.2 0.6 fusion.12
  145.8 0.5 copy-done.4
  146.2 0.5 fusion.43
  146.7 0.5 fusion.45
  147.2 0.5 fusion.47
  147.7 0.5 fusion.49
  148.2 2.5 fusion.8
  150.8 1.0 copy-done.6
  151.8 2.6 convolution_bitcast_fusion.1.mine
  154.4 5.3 %shard_map.255 = f32[1088,256]{1,0:T(8,128)} custom-call(f32[1088,256]{1,0:T(8,128)} %convolution_bitcast_fusion.1.mine), custom_call_target="tpu_custom_call" | custom-call | tf_op jit(solution)/shard_map/pallas_call | solution.py:326
  159.8 2.1 multiply_reduce_fusion
  161.9 1.4 fusion.75
  163.3 0.1 stack.56
  163.4 0.1 stack.55
  163.6 0.1 stack.57
  163.7 0.2 reshape.116
  163.9 3.2 %fusion.1 = bf16[1088,256]{1,0:T(8,128)(2,1)S(1)} fusion(bf16[32,48,1088]{2,1,0:T(8,128)(2,1)} %bitcast.214, bf16[32,34,256]{2,1,0:T(8,128)(2,1)S(1)} %reshape.116), kind=kOutput, calls=%fused_computation.7 | convolution fusion | flops 855916544 | bytes 4456448 | tf_op jit(solution)/shard_map/ced,cet->dt/dot_general | solution.py:1344
  167.2 0.8 pad_maximum_fusion.1.send
  168.0 0.2 copy.55
  168.2 0.1 copy-done.20
  168.4 2.0 fusion
  170.4 0.2 reshape.118
  170.5 0.9 pad.67.wide
  171.5 0.5 copy-done.7
  171.9 4.2 %convolution_convert_fusion = bf16[16,144,1152]{2,1,0:T(8,128)(2,1)} fusion(bf16[16,144,256]{2,1,0:T(8,128)(2,1)S(1)} %copy-done.7, bf16[1088,256]{1,0:T(8,128)(2,1)S(1)} %copy-done.9, bf16[1152]{0:T(1024)(128)(2,1)S(1)} %pad.80.clone), kind=kOutput, calls=%fused_computation | convolution fusion | flops 1362788352 | bytes 7047424 | tf_op jit(solution)/shard_map/xft,dt->xfd/dot_general | solution.py:1337
  176.1 127.5 %shard_map.256 = (bf16[32,48,256]{2,1,0:T(8,128)(2,1)}, bf16[16,48,256]{2,1,0:T(8,128)(2,1)}, f32[304,384]{1,0:T(8,128)}, f32[304,128]{1,0:T(8,128)}, f32[1,160,256]{2,1,0:T(8,128)}, /*index=5*/f32[48,128]{1,0:T(8,128)}) custom-call(bf16[4,3,1,64,256]{4,3,2,1,0:T(8,128)(2,1)} %pad_maximum_fusion.1.send, s32[1,1024]{1,0:T(1,128)} %constant_dynamic-slice_fusion.2.seg_row_ref, ...), custom_call_target="tpu_custom_call" | custom-call | tf_op jit(solution)/shard_map/pallas_call | solution.py:1157
  303.7 1.4 convert_reduce_fusion.1
  305.1 0.2 copy.57
  305.3 0.7 slice_reduce_fusion.1
  306.0 0.8 slice_reduce_fusion.3
  306.8 0.6 pad_maximum_fusion.3
  307.3 0.7 slice_reduce_fusion.5
  308.2 0.7 pad_maximum_fusion.2
  308.9 0.7 dynamic-slice_bitcast_fusion.1
  309.6 0.4 copy.68
  310.0 1.0 broadcast_add_fusion
  311.0 0.1 dynamic-slice
  311.1 0.8 dynamic-slice_bitcast_fusion
  311.9 0.7 reshape.123
  312.7 0.2 copy.58
  312.9 1.2 copy.69
  (76 shorter events, 0.8 us)
Async XLA Ops:
  0.6 2.9 copy-start
  0.7 7.0 %copy-start.16 = (bf16[272,136]{0,1:T(8,128)(2,1)S(1)}, bf16[272,136]{0,1:T(8,128)(2,1)}, u32[]{:S(2)}) copy-start(bf16[272,136]{0,1:T(8,128)(2,1)} %param.22) | copy-start | bytes 221956
  0.7 7.0 %copy-start.18 = (bf16[272,34]{0,1:T(8,128)(2,1)S(1)}, bf16[272,34]{0,1:T(8,128)(2,1)}, u32[]{:S(2)}) copy-start(bf16[272,34]{0,1:T(8,128)(2,1)} %param.20) | copy-start | bytes 55492
  0.7 7.7 %copy-start.11 = (bf16[34,4096]{1,0:T(8,128)(2,1)S(1)}, bf16[34,4096]{1,0:T(8,128)(2,1)}, u32[]{:S(2)}) copy-start(bf16[34,4096]{1,0:T(8,128)(2,1)} %param.15) | copy-start | bytes 835588
  0.7 8.5 %copy-start.12 = (bf16[34,4096]{1,0:T(8,128)(2,1)S(1)}, bf16[34,4096]{1,0:T(8,128)(2,1)}, u32[]{:S(2)}) copy-start(bf16[34,4096]{1,0:T(8,128)(2,1)} %param.16) | copy-start | bytes 835588
  133.9 4.5 %copy-start.9 = (bf16[1088,256]{1,0:T(8,128)(2,1)S(1)}, bf16[1088,256]{1,0:T(8,128)(2,1)}, u32[]{:S(2)}) copy-start(bf16[1088,256]{1,0:T(8,128)(2,1)} %get-tuple-element.42) | copy-start | bytes 1671172
  135.8 6.8 %slice-start = ((s8[5242880]{0:T(1024)(128)(4,1)}), s8[4194304]{0:T(1024)(128)(4,1)S(1)}, s32[]{:S(2)}) async-start(s8[5242880]{0:T(1024)(128)(4,1)} %bitcast.181), calls=%async_computation | async-start | bytes 8388608
  138.3 4.3 %slice-start.1 = ((s8[5242880]{0:T(1024)(128)(4,1)}), s8[1048576]{0:T(1024)(128)(4,1)S(1)}, s32[]{:S(2)}) async-start(s8[5242880]{0:T(1024)(128)(4,1)} %bitcast.181), calls=%async_computation.1 | async-start | bytes 2097152
  142.6 2.6 copy-start.2
  145.2 1.1 copy-start.4
  147.7 4.1 %slice-start.2 = ((s8[5308416]{0:T(1024)(128)(4,1)}), s8[4194304]{0:T(1024)(128)(4,1)S(1)}, s32[]{:S(2)}) async-start(s8[5308416]{0:T(1024)(128)(4,1)} %bitcast.211), calls=%async_computation.2 | async-start | bytes 8388608
  148.2 3.6 %slice-start.3 = ((s8[5308416]{0:T(1024)(128)(4,1)}), s8[1114112]{0:T(1024)(128)(4,1)S(1)}, s32[]{:S(2)}) async-start(s8[5308416]{0:T(1024)(128)(4,1)} %bitcast.211), calls=%async_computation.3 | async-start | bytes 2228224
  150.8 1.0 copy-start.6
  154.4 5.3 %copy-start.5 = (f32[1088,256]{1,0:T(8,128)S(1)}, f32[1088,256]{1,0:T(8,128)}, u32[]{:S(2)}) copy-start(f32[1088,256]{1,0:T(8,128)} %get-tuple-element.45) | copy-start | bytes 3342340
  154.4 5.3 %copy-start.8 = (f32[1088,256]{1,0:T(8,128)S(1)}, f32[1088,256]{1,0:T(8,128)}, u32[]{:S(2)}) copy-start(f32[1088,256]{1,0:T(8,128)} %get-tuple-element.49) | copy-start | bytes 3342340
  159.8 2.1 copy-start.3
  159.8 2.1 copy-start.19
  167.2 1.2 copy-start.20
  170.4 1.6 copy-start.7
  303.7 1.6 copy-start.14
  303.7 3.7 %copy-start.17 = (f32[48,128]{1,0:T(8,128)S(1)}, f32[48,128]{1,0:T(8,128)}, u32[]{:S(2)}) copy-start(f32[48,128]{1,0:T(8,128)} %get-tuple-element.59) | copy-start | bytes 73732
  303.7 4.4 %copy-start.15 = (f32[1,160,256]{2,1,0:T(8,128)S(1)}, f32[1,160,256]{2,1,0:T(8,128)}, u32[]{:S(2)}) copy-start(f32[1,160,256]{2,1,0:T(8,128)} %get-tuple-element.58) | copy-start | bytes 491524
  305.1 3.8 %copy-start.10 = (f32[304,384]{1,0:T(8,128)S(1)}, f32[304,384]{1,0:T(8,128)}, u32[]{:S(2)}) copy-start(f32[304,384]{1,0:T(8,128)} %get-tuple-element.56) | copy-start | bytes 1400836
  310.0 2.6 copy-start.13
  312.7 1.5 copy-start.1
where the time goes:
time: 315 us; the launch traced here: 314 us
  Pallas kernels  256 us (81%)
  matrix products  23.3 us (7%)
  local copies, waits for them, and re-layouts  23 us (7%)
  other arithmetic  10.9 us (3%)
    pallas_call x1, Pallas kernels, attend_back(): pl.pallas_call(back_kernel, in_specs=[VMEM] * 6 + [ANY] + [VMEM] * 4 + [A...  128 us
    pallas_call x1, Pallas kernels, front(): pl.pallas_call(front_kernel, in_specs=[ANY, ANY, VMEM, ANY, VMEM, VMEM],...  123 us

commit v1 on v0

--- a/solution.py
+++ b/solution.py
@@ -319,7 +319,7 @@
     copy = remote(mine, got, send, recv, partner)
     copy.start()
     copy.wait()
-    total[...] = mine[...] + got[...]
+    total[...] = mine[...].astype(F32) + got[...].astype(F32)
 
 
 def core_sum(mine):
@@ -328,7 +328,7 @@
         in_specs=[VMEM],
         out_specs=VMEM,
         out_shape=jax.ShapeDtypeStruct(mine.shape, F32),
-        scratch_shapes=[pltpu.VMEM(mine.shape, F32), DMA, DMA],
+        scratch_shapes=[pltpu.VMEM(mine.shape, mine.dtype), DMA, DMA],
         compiler_params=params(4),
     )(mine)
 
@@ -621,7 +621,6 @@
 
     a_middle(1, swap)
     f_begin(1)
-    g_begin()
     a_finish(1, swap)
     for out, come in swaps:
         come.wait_recv()
@@ -661,6 +660,8 @@
 
         lax.fori_loop(0, 4, heads, 0)
         begin(slot)
+
+    g_begin()
 
     def unit(slot, _):
         arrive(slot)
@@ -704,7 +705,8 @@
 
     lax.fori_loop(0, 8, project_out, 0)
     normed2, standard2, inv_std2 = norm_in(resid_ref[...], vector(5), vector(6))
-    normed2_ref[...] = normed2
+    normed2_ref[:full] = normed2
+    normed2_ref[full:] = ones_row
     standard2_ref[...] = standard2
     inv_std2_ref[...] = inv_std2
     g_end()
@@ -750,7 +752,7 @@
             jax.ShapeDtypeStruct((3, 1, length), F32),
             low,
             flat,
-            low,
+            jax.ShapeDtypeStruct((WIDE, 256), BF16),
             flat,
             stat,
             jax.ShapeDtypeStruct((full, 16), F32),
@@ -808,7 +810,8 @@
     lse_ref,
     wide,
     out_in,
-    up_in,
+    dhidden_ref,
+    normed2_ref,
     active_ref,
     g_ref,
     qkv_w,
@@ -817,12 +820,16 @@
     inv_std_ref,
     gain_ref,
     dresid_ref,
-    wide_out,
+    bias_ref,
+    layer_out,
     input_out,
     main_out,
     tail_out,
     down_out,
     column_out,
+    wide_got,
+    input_got,
+    up_in,
     down_in,
     grad_ref,
     dqkv_ref,
@@ -879,6 +886,13 @@
     )
     for slot in range(3):
         begin(slot)
+
+    def up_part(slab, _):
+        part = nt(dhidden_ref[slab], normed2_ref[...])
+        up_in[slab // 4, slab % 4] = part.astype(BF16)
+        return 0
+
+    lax.fori_loop(0, 16, up_part, 0)
     first[0](0)
 
     tail_rows = g_ref.shape[0] // 4 - DOWN_MAIN
@@ -901,22 +915,18 @@
 
     down_part((iz + 2) % 4)
     down[0](0, (0, 1))
-    down_part((iz + 1) % 4)
-    down_part((iz + 3) % 4)
-    down[0](0, (2, 3))
 
     def copy_wide(step, owner):
         peer = (place + step) % 32
         return remote(
-            wide.at[peer], wide_out.at[owner], wsend.at[step], wrecv.at[step], col_device(peer)
+            wide.at[peer], wide_got.at[owner], wsend.at[step], wrecv.at[step], col_device(peer)
         )
 
     def begin_wide(step, _):
         copy_wide(step, place).start()
         return 0
 
-    lax.fori_loop(1, 32, begin_wide, 0)
-    own = pltpu.make_async_copy(wide.at[place], wide_out.at[place], local)
+    own = pltpu.make_async_copy(wide.at[place], wide_got.at[place], local)
     own.start()
 
     def copy_w(step):
@@ -955,8 +965,12 @@
 
     lax.fori_loop(0, count, unit, 0)
     first[1](0)
+    down_part((iz + 1) % 4)
+    down_part((iz + 3) % 4)
+    down[0](0, (2, 3))
     down[1](0)
     down_part(iz)
+    lax.fori_loop(1, 32, begin_wide, 0)
     sent()
     pass_on()
     finish(count)
@@ -1005,6 +1019,7 @@
         return 0
 
     lax.fori_loop(0, 8, product, 0)
+    last[1](0)
     first[2](0)
     first[0](1)
 
@@ -1048,7 +1063,7 @@
         peer = (xy + step) % 16
         return remote(
             input_slabs.at[peer * 2 + core],
-            input_out.at[owner],
+            input_got.at[owner],
             isend.at[step],
             irecv.at[step],
             {"x": peer // 4, "y": peer % 4},
@@ -1068,7 +1083,7 @@
         return 0
 
     lax.fori_loop(1, 16, begin_input, 0)
-    input_out[xy] = input_slabs[xy * 2 + core]
+    input_got[xy] = input_slabs[xy * 2 + core]
 
     def z_columns(step):
         return remote(
@@ -1096,7 +1111,6 @@
 
     first[1](1)
     down[1](1)
-    last[1](0)
     first[2](1)
     begin_z(0)
     cols[1](0)
@@ -1127,11 +1141,24 @@
 
     lax.fori_loop(1, 32, end_wide, 0)
 
+    def put_layer(chip, _):
+        halves = wide_got[chip * 2, :34].astype(F32) + wide_got[chip * 2 + 1, :34].astype(F32)
+        layer_out[:, rows_of(chip * 256)] = halves + bias_ref[...]
+        return 0
+
+    lax.fori_loop(0, 16, put_layer, 0)
+
     def end_input(step, _):
         copy_input(step, (xy + 16 - step) % 16).wait()
         return 0
 
     lax.fori_loop(1, 16, end_input, 0)
+
+    def put_input(chip, _):
+        input_out[:, rows_of(chip * 256)] = input_got[chip, :34].astype(F32)
+        return 0
+
+    lax.fori_loop(0, 16, put_input, 0)
     for group in range(2):
         for step in range(1, 4):
             for c in z_copies(group, step):
@@ -1145,7 +1172,7 @@
 
 
 def attend_back(
-    send, seg_row, seg_col, qkv, out, lse, wide, out_part, up_part, active, g, qkv_w, normed, standard, inv_std, gain, dresid
+    send, seg_row, seg_col, qkv, out, lse, wide, out_part, dhidden, normed2, active, g, qkv_w, normed, standard, inv_std, gain, dresid, bias
 ):
     length = seg_row.shape[1]
     full = qkv_w.shape[-1]
@@ -1156,17 +1183,20 @@
     total = sum(SUM_ROWS)
     return pl.pallas_call(
         back_kernel,
-        in_specs=[VMEM] * 6 + [ANY] + [VMEM] * 4 + [ANY, VMEM, ANY, VMEM, VMEM, ANY],
-        out_specs=[ANY] + [VMEM] * 5,
+        in_specs=[VMEM] * 6 + [ANY] + [VMEM] * 5 + [ANY, VMEM, ANY, VMEM, VMEM, ANY, VMEM],
+        out_specs=[VMEM] * 6,
         out_shape=[
-            jax.ShapeDtypeStruct(wide.shape, wide.dtype),
-            jax.ShapeDtypeStruct((16, 48, 256), BF16),
+            jax.ShapeDtypeStruct((34, 4096), F32),
+            jax.ShapeDtypeStruct((34, 4096), F32),
             jax.ShapeDtypeStruct((total, WINDOW), F32),
             jax.ShapeDtypeStruct((total, LANE), F32),
             jax.ShapeDtypeStruct((1, DOWN_ROWS, DOWN_MAIN), F32),
             jax.ShapeDtypeStruct((48, LANE), F32),
         ],
         scratch_shapes=[
+            pltpu.VMEM(wide.shape, BF16),
+            pltpu.VMEM((16, 48, 256), BF16),
+            pltpu.VMEM((4, 4, FF_ROWS, WIDE), BF16),
             pltpu.VMEM((4, 16, DOWN_ROWS, DOWN_MAIN), BF16),
             pltpu.VMEM((3, 1, HD, length), BF16),
             pltpu.VMEM((3, 3, HD, length), BF16),
@@ -1212,7 +1242,7 @@
         + column_bufs,
         compiler_params=params(6, 62),
     )(
-        send, seg_row, seg_col, qkv, out, lse, wide, out_part, up_part, active, g, qkv_w, normed, standard, inv_std, gain, dresid
+        send, seg_row, seg_col, qkv, out, lse, wide, out_part, dhidden, normed2, active, g, qkv_w, normed, standard, inv_std, gain, dresid, bias
     )
 
 
@@ -1310,7 +1340,7 @@
         qkv_w[:, 3 * width, :units].reshape(16, 2, units), core, 1, keepdims=False
     ).astype(F32)
     hidden_bias = jnp.pad(hidden_bias, ((0, 0), (0, FF_ROWS - units)))
-    hidden = jnp.einsum("xfd,dt->xft", up_w, normed2, preferred_element_type=F32) + hidden_bias[..., None]
+    hidden = jnp.einsum("xfd,dt->xft", up_w, normed2[:full], preferred_element_type=F32) + hidden_bias[..., None]
     active, gelu_back = jax.vjp(lambda h: jax.nn.gelu(h, approximate=True), hidden)
     active = active.astype(BF16)
     active_rows = jnp.pad(active, ((0, 0), (0, DOWN_ROWS - FF_ROWS), (0, 0)))
@@ -1334,9 +1364,8 @@
     def widen(v):
         return jnp.concatenate([v, ones_row], 0)
 
-    up_part = jnp.einsum("xft,dt->xfd", dhidden, widen(normed2), preferred_element_type=F32).astype(BF16)
     dn2 = jnp.einsum("xfd,xft->dt", up_w, dhidden, preferred_element_type=F32)
-    dn2 = core_sum(dn2)
+    dn2 = core_sum(dn2.astype(BF16))
     back2, gain2_grad, shift2_grad = norm_back(dn2, standard2, inv_std2, gain2)
     dresid = g + back2
     dproj = dresid.astype(BF16)
@@ -1347,7 +1376,7 @@
     cols = lax.dynamic_index_in_dim(cols, core, 1, keepdims=False)
     cols = jnp.pad(cols, ((0, 0), (0, OUT_ROWS - width), (full + 1, extra - 4)))
     out_part = jnp.einsum("xrt,dt->xrd", mine, widen(attn), preferred_element_type=F32) + cols
-    got_out, input_got, main, tail, down_sum, columns = attend_back(
+    layer_output, input_grad, main, tail, down_sum, columns = attend_back(
         to_heads(dattn[None], core),
         seg_row,
         seg_col,
@@ -1356,7 +1385,8 @@
         lse,
         send_out,
         out_part.astype(BF16).reshape(4, 4, OUT_ROWS, WIDE),
-        up_part.reshape(4, 4, FF_ROWS, WIDE),
+        dhidden,
+        normed2,
         active,
         g_low,
         qkv_w,
@@ -1365,11 +1395,8 @@
         inv_std1,
         gain1,
         dresid,
-    )
-    layer_output = jnp.sum(got_out[:, :width].reshape(16, 2, width, 256).astype(F32), 1)
-    layer_output = layer_output.transpose(1, 0, 2).reshape(width, 4096)
-    layer_output = layer_output + down_bias.astype(F32)[:, None]
-    input_grad = input_got[:, :width].transpose(1, 0, 2).reshape(width, 4096).astype(F32)
+        down_bias.astype(F32)[:, None],
+    )
     main = lax.dynamic_slice_in_dim(main, lax.axis_index("row") * (rows - 256), rows, 1)
     out_first, up_first, qkv_first = SUM_FIRST
     qkv_out = main[qkv_first : qkv_first + 3 * width].reshape(3, width, rows).transpose(2, 0, 1)

time: 315 us -> 303 us (0.962)
  matrix products: 23.3 us -> 17.2 us
  Pallas kernels: 256 us -> 250 us
    pallas_call x1, Pallas kernels: 128 us -> 121 us  [attend_back(): pl.pallas_call(back_kernel, in_specs=[VMEM] * 6 + [ANY] + [VMEM] * 5 + [A...]
    dot_general x2 -> x1, matrix products: 8.46 us -> 4.24 us  [shards(): jnp.einsum('xfd,dt->xft', up_w, normed2[:full], preferred_element_type=F32)]
where the time goes in v1:
time: 303 us; the launch traced here: 301 us
  Pallas kernels  250 us (83%)
  local copies, waits for them, and re-layouts  23.7 us (8%)
  matrix products  17.2 us (6%)
  other arithmetic  9.02 us (3%)
    pallas_call x1, Pallas kernels, front(): pl.pallas_call(front_kernel, in_specs=[ANY, ANY, VMEM, ANY, VMEM, VMEM],...  124 us
    pallas_call x1, Pallas kernels, attend_back(): pl.pallas_call(back_kernel, in_specs=[VMEM] * 6 + [ANY] + [VMEM] * 5 + [A...  121 us

profile of v1, /device:TPU:0, one launch (start us, length us, event | category | flops | bytes accessed | tf_op | source)
XLA Modules:
  0.0 300.7 jit_solution(17780896245184214274)
XLA Ops:
  0.6 0.0 copy-start
  0.7 0.7 copy-done
  1.4 0.0 copy-start.16
  1.4 1.0 copy.36.seg_col_ref
  2.4 0.6 constant_dynamic-slice_fusion.2.seg_row_ref
  3.0 0.8 concatenate.25
  3.8 0.0 slice-start.3
  3.9 0.8 pad_maximum_fusion.x_src
  4.7 0.8 pad.55.g_src
  5.6 0.7 fusion.39.block
  6.3 0.1 copy.49
  6.4 0.7 fusion.55.down_block
  7.0 124.4 %shard_map.254 = (bf16[4,4,2,112,1088]{4,3,2,1,0:T(8,128)(2,1)}, bf16[4,4,2,48,1088]{4,3,2,1,0:T(8,128)(2,1)}, bf16[4,4,144,1088]{3,2,1,0:T(8,128)(2,1)}, bf16[4...) custom-call(bf16[48,4096]{1,0:T(8,128)(2,1)} %pad_maximum_fusion.x_s, ...), custom_call_target="tpu_custom_call" | custom-call | tf_op jit(solution)/shard_map/pallas_call | solution.py:737
  131.4 1.1 slice_reduce_fusion.2
  132.6 4.2 %multiply_convert_fusion = (bf16[16,144,256]{2,1,0:T(8,128)(2,1)S(1)}, f32[16,144,256]{2,1,0:T(8,128)S(1)}) fusion(f32[16,144]{1,0:T(8,128)S(1)} %pad_convert_fusion, bf16[16,144,1088]{2,1,0:T(8,128)(2,1)} %bitcast.192, bf16[1152,256]{1,0:T(8,128)(2,1)} %get-tuple-element.42.normed2_ref), kind=kOutput, calls=%fused_computation.19 | convolution fusion | flops 1289355264 | bytes 9413632 | tf_op jit(solution)/shard_map/xfd,dt->xft/dot_general | solution.py:1343
  136.9 0.4 fusion.17
  137.3 0.3 fusion.75
  137.6 0.5 fusion.16
  138.2 0.6 fusion.15
  138.8 0.6 fusion.14
  139.4 0.6 fusion.13
  139.9 0.5 copy-done.4
  140.4 0.5 fusion.49
  140.9 0.5 fusion.47
  141.4 0.5 fusion.45
  141.9 0.5 fusion.43
  142.5 2.7 fusion.9.dhidden_ref
  145.2 1.0 copy-done.9
  146.2 2.4 fusion.2.mine
  148.6 4.3 %shard_map.255 = f32[1088,256]{1,0:T(8,128)} custom-call(bf16[1088,256]{1,0:T(8,128)(2,1)} %fusion.2.mine), custom_call_target="tpu_custom_call" | custom-call | tf_op jit(solution)/shard_map/pallas_call | solution.py:326
  152.9 1.2 fusion.76
  154.1 0.1 copy-done.3
  154.1 3.1 %multiply_reduce_fusion = (f32[1088]{0:T(1024)S(1)}, f32[256]{0:T(256)S(1)}, f32[256]{0:T(256)S(1)}, f32[1088]{0:T(1024)S(1)}, bf16[1088,256]{1,0:T(8,128)(2,1)}) fusion(f32[1088,256]{1,0:T(8,128)S(1)} %copy-done.3, f32[1088,256]{1,0:T(8,128)S(1)} %copy-done.5, f32[1088]{0:T(1024)S(1)} %get-tuple-element.79, f32[1088,256]{1,0:T(8,128)} %copy-done.8, ...), kind=kLoop, calls=%fused_computation.33 | loop fusion | flops 2782592 | bytes 5028612 | tf_op jit(solution)/shard_map/reduce_sum | solution.py:1254
  157.2 1.6 fusion.74
  158.9 0.1 stack.55
  159.0 0.1 stack.56
  159.1 0.1 stack.57
  159.2 0.2 copy.40
  159.5 1.3 reshape.103
  160.8 0.1 pad.63
  160.9 0.1 pad.76.clone
  161.0 2.1 fusion
  163.1 0.5 copy-done.21
  163.6 1.2 fusion.1
  164.9 0.8 pad_maximum_fusion.1.send
  165.7 0.1 copy-done.6
  165.8 0.2 reshape.105
  166.0 0.9 pad.65.wide
  166.9 0.7 copy.42.bias_ref
  167.6 121.0 %shard_map.256 = (f32[34,4096]{1,0:T(8,128)}, f32[34,4096]{1,0:T(8,128)}, f32[304,384]{1,0:T(8,128)}, f32[304,128]{1,0:T(8,128)}, f32[1,160,256]{2,1,0:T(8,128)}, /*index=5*/f32[48,128]{1,0:T(8,128)}) custom-call(bf16[4,3,1,64,256]{4,3,2,1,0:T(8,128)(2,1)} %pad_maximum_fusion.1.send, s32[1,1024]{1,0:T(1,128)} %constant_dynamic-slice_fusion.2.seg_row_ref, ...), custom_call_target="tpu_custom_call" | custom-call | tf_op jit(solution)/shard_map/pallas_call | solution.py:1184
  288.6 1.0 slice_bitcast_fusion
  289.6 0.7 slice_bitcast_fusion.5
  290.4 0.1 copy.43
  290.5 0.7 pad_maximum_fusion.2
  291.2 1.6 slice_reduce_fusion.3
  292.8 0.6 pad_maximum_fusion.3
  293.4 1.1 dynamic-slice
  294.5 0.7 reshape.108
  295.2 0.8 dynamic-slice_bitcast_fusion
  296.0 0.7 dynamic-slice_bitcast_fusion.1
  296.7 0.7 slice_reduce_fusion.5
  297.4 1.6 slice_reduce_fusion.1
  299.0 0.8 copy.65
  299.9 0.8 copy.66
  (79 shorter events, 0.4 us)
Async XLA Ops:
  0.6 0.7 copy-start
  0.7 3.2 %copy-start.13 = (bf16[34,4096]{1,0:T(8,128)(2,1)S(1)}, bf16[34,4096]{1,0:T(8,128)(2,1)}, u32[]{:S(2)}) copy-start(bf16[34,4096]{1,0:T(8,128)(2,1)} %param.15) | copy-start | bytes 835588
  0.7 4.0 %copy-start.14 = (bf16[34,4096]{1,0:T(8,128)(2,1)S(1)}, bf16[34,4096]{1,0:T(8,128)(2,1)}, u32[]{:S(2)}) copy-start(bf16[34,4096]{1,0:T(8,128)(2,1)} %param.16) | copy-start | bytes 835588
  1.4 4.1 %copy-start.16 = (bf16[272,3,34]{0,2,1:T(8,128)(2,1)S(1)}, bf16[272,3,34]{0,2,1:T(8,128)(2,1)}, u32[]{:S(2)}) copy-start(bf16[272,3,34]{0,2,1:T(8,128)(2,1)} %param.18) | copy-start | bytes 166468
  2.4 3.1 %copy-start.23 = (bf16[136]{0:T(256)(128)(2,1)S(1)}, bf16[136]{0:T(256)(128)(2,1)}, u32[]{:S(2)}) copy-start(bf16[136]{0:T(256)(128)(2,1)} %param.23) | copy-start | bytes 820
  2.4 3.1 %copy-start.15 = (bf16[272,136]{0,1:T(8,128)(2,1)S(1)}, bf16[272,136]{0,1:T(8,128)(2,1)}, u32[]{:S(2)}) copy-start(bf16[272,136]{0,1:T(8,128)(2,1)} %param.22) | copy-start | bytes 221956
  2.4 3.1 %copy-start.18 = (bf16[272,34]{0,1:T(8,128)(2,1)S(1)}, bf16[272,34]{0,1:T(8,128)(2,1)}, u32[]{:S(2)}) copy-start(bf16[272,34]{0,1:T(8,128)(2,1)} %param.20) | copy-start | bytes 55492
  3.8 2.5 slice-start.3
  3.8 2.5 slice-start.2
  131.4 5.5 %slice-start = ((s8[5242880]{0:T(1024)(128)(4,1)}), s8[1048576]{0:T(1024)(128)(4,1)S(1)}, s32[]{:S(2)}) async-start(s8[5242880]{0:T(1024)(128)(4,1)} %bitcast.168), calls=%async_computation | async-start | bytes 2097152
  132.6 4.3 %slice-start.1 = ((s8[5242880]{0:T(1024)(128)(4,1)}), s8[4194304]{0:T(1024)(128)(4,1)S(1)}, s32[]{:S(2)}) async-start(s8[5242880]{0:T(1024)(128)(4,1)} %bitcast.168), calls=%async_computation.1 | async-start | bytes 8388608
  136.9 2.5 copy-start.2
  139.4 1.1 copy-start.4
  139.9 1.5 copy-start.8
  141.9 4.3 %slice-start.4 = ((s8[5308416]{0:T(1024)(128)(4,1)}), s8[4194304]{0:T(1024)(128)(4,1)S(1)}, s32[]{:S(2)}) async-start(s8[5308416]{0:T(1024)(128)(4,1)} %bitcast.193), calls=%async_computation.4 | async-start | bytes 8388608
  142.5 3.7 %slice-start.5 = ((s8[5308416]{0:T(1024)(128)(4,1)}), s8[1114112]{0:T(1024)(128)(4,1)S(1)}, s32[]{:S(2)}) async-start(s8[5308416]{0:T(1024)(128)(4,1)} %bitcast.193), calls=%async_computation.5 | async-start | bytes 2228224
  145.2 1.0 copy-start.9
  148.6 4.3 %copy-start.7 = (f32[1088,16]{1,0:T(8,128)S(1)}, f32[1088,16]{1,0:T(8,128)}, u32[]{:S(2)}) copy-start(f32[1088,16]{1,0:T(8,128)} %get-tuple-element.44) | copy-start | bytes 208900
  148.6 5.4 %copy-start.5 = (f32[1088,256]{1,0:T(8,128)S(1)}, f32[1088,256]{1,0:T(8,128)}, u32[]{:S(2)}) copy-start(f32[1088,256]{1,0:T(8,128)} %get-tuple-element.45) | copy-start | bytes 3342340
  152.9 1.2 copy-start.3
  154.1 3.1 %copy-start.19 = (f32[1,256]{1,0:T(1,128)S(1)}, f32[1,256]{1,0:T(1,128)}, u32[]{:S(2)}) copy-start(f32[1,256]{1,0:T(1,128)} %get-tuple-element.39) | copy-start | bytes 3076
  159.5 1.4 copy-start.20
  159.5 1.5 copy-start.22
  161.0 2.6 copy-start.21
  164.8 1.1 copy-start.6
  165.8 1.1 copy-start.24
  288.6 6.6 %copy-start.12 = (f32[304,384]{1,0:T(8,128)S(1)}, f32[304,384]{1,0:T(8,128)}, u32[]{:S(2)}) copy-start(f32[304,384]{1,0:T(8,128)} %get-tuple-element.56) | copy-start | bytes 1400836
  288.6 8.1 %copy-start.17 = (f32[48,128]{1,0:T(8,128)S(1)}, f32[48,128]{1,0:T(8,128)}, u32[]{:S(2)}) copy-start(f32[48,128]{1,0:T(8,128)} %get-tuple-element.59) | copy-start | bytes 73732
  288.6 10.4 %copy-start.11 = (f32[34,4096]{1,0:T(8,128)S(1)}, f32[34,4096]{1,0:T(8,128)}, u32[]{:S(2)}) copy-start(f32[34,4096]{1,0:T(8,128)} %get-tuple-element.102) | copy-start | bytes 1671172
  293.4 6.5 %copy-start.10 = (f32[34,4096]{1,0:T(8,128)S(1)}, f32[34,4096]{1,0:T(8,128)}, u32[]{:S(2)}) copy-start(f32[34,4096]{1,0:T(8,128)} %get-tuple-element.103) | copy-start | bytes 1671172
  297.4 3.3 %copy-start.1 = (s32[4,1024]{1,0:T(4,128)S(1)}, s32[4,1024]{1,0:T(4,128)}, u32[]{:S(2)}) copy-start(s32[4,1024]{1,0:T(4,128)} %param.17) | copy-start | bytes 49156

commit v2 on v1

--- a/solution.py
+++ b/solution.py
@@ -995,14 +995,19 @@
 
     lax.fori_loop(0, 8, by_slab, 0)
 
-    def weight_part(step, _):
-        index = step * 2 + core
-        part = nt(slabs[index], normed_ref[...])
-        qkv_part[step // 4, step % 4] = part.astype(BF16)
-        return 0
-
-    lax.fori_loop(0, 16, weight_part, 0)
-    last[0](0)
+    far_x, far_y = (ix + 2) % 4, (iy + 2) % 4
+
+    def weight_part(dx, dy):
+        px, py = (far_x + dx) % 4, (far_y + dy) % 4
+        part = nt(slabs[(px * 4 + py) * 2 + core], normed_ref[...])
+        qkv_part[px, py] = part.astype(BF16)
+        return 0
+
+    lax.fori_loop(0, 4, lambda step, _: weight_part(step, 0), 0)
+    lax.fori_loop(1, 4, lambda step, _: weight_part(0, step), 0)
+    last[0](0, (0, 1))
+    lax.fori_loop(0, 9, lambda step, _: weight_part(1 + step // 3, 1 + step % 3), 0)
+    last[0](0, (2, 3))
 
     def product(step, _):
         @pl.when(step < 7)

time: 303 us -> 300 us (0.990)
  no operation moved by 1% of the time
where the time goes in v2:
time: 300 us; the launch traced here: 298 us
  Pallas kernels  247 us (82%)
  local copies, waits for them, and re-layouts  23.7 us (8%)
  matrix products  17.2 us (6%)
  other arithmetic  9.02 us (3%)
    pallas_call x1, Pallas kernels, front(): pl.pallas_call(front_kernel, in_specs=[ANY, ANY, VMEM, ANY, VMEM, VMEM],...  124 us
    pallas_call x1, Pallas kernels, attend_back(): pl.pallas_call(back_kernel, in_specs=[VMEM] * 6 + [ANY] + [VMEM] * 5 + [A...  118 us

profile of v2, /device:TPU:0, one launch (start us, length us, event | category | flops | bytes accessed | tf_op | source)
XLA Modules:
  0.0 297.8 jit_solution(12128541297306823385)
XLA Ops:
  0.6 0.0 copy-start
  0.7 0.7 copy-done
  1.4 0.0 copy-start.16
  1.4 1.0 copy.36.seg_col_ref
  2.4 0.6 constant_dynamic-slice_fusion.2.seg_row_ref
  3.0 0.8 concatenate.25
  3.8 0.0 slice-start.3
  3.9 0.8 pad_maximum_fusion.x_src
  4.7 0.8 pad.55.g_src
  5.6 0.7 fusion.39.block
  6.3 0.1 copy.49
  6.4 0.7 fusion.55.down_block
  7.0 124.4 %shard_map.254 = (bf16[4,4,2,112,1088]{4,3,2,1,0:T(8,128)(2,1)}, bf16[4,4,2,48,1088]{4,3,2,1,0:T(8,128)(2,1)}, bf16[4,4,144,1088]{3,2,1,0:T(8,128)(2,1)}, bf16[4...) custom-call(bf16[48,4096]{1,0:T(8,128)(2,1)} %pad_maximum_fusion.x_s, ...), custom_call_target="tpu_custom_call" | custom-call | tf_op jit(solution)/shard_map/pallas_call | solution.py:737
  131.4 1.1 slice_reduce_fusion.2
  132.6 4.2 %multiply_convert_fusion = (bf16[16,144,256]{2,1,0:T(8,128)(2,1)S(1)}, f32[16,144,256]{2,1,0:T(8,128)S(1)}) fusion(f32[16,144]{1,0:T(8,128)S(1)} %pad_convert_fusion, bf16[16,144,1088]{2,1,0:T(8,128)(2,1)} %bitcast.192, bf16[1152,256]{1,0:T(8,128)(2,1)} %get-tuple-element.42.normed2_ref), kind=kOutput, calls=%fused_computation.19 | convolution fusion | flops 1289355264 | bytes 9413632 | tf_op jit(solution)/shard_map/xfd,dt->xft/dot_general | solution.py:1348
  136.9 0.4 fusion.17
  137.3 0.3 fusion.75
  137.6 0.5 fusion.16
  138.2 0.6 fusion.15
  138.8 0.6 fusion.14
  139.4 0.6 fusion.13
  139.9 0.5 copy-done.4
  140.4 0.5 fusion.49
  140.9 0.5 fusion.47
  141.4 0.5 fusion.45
  141.9 0.5 fusion.43
  142.5 2.7 fusion.9.dhidden_ref
  145.2 1.0 copy-done.9
  146.2 2.4 fusion.2.mine
  148.6 4.3 %shard_map.255 = f32[1088,256]{1,0:T(8,128)} custom-call(bf16[1088,256]{1,0:T(8,128)(2,1)} %fusion.2.mine), custom_call_target="tpu_custom_call" | custom-call | tf_op jit(solution)/shard_map/pallas_call | solution.py:326
  152.9 1.2 fusion.76
  154.1 0.1 copy-done.3
  154.1 3.1 %multiply_reduce_fusion = (f32[1088]{0:T(1024)S(1)}, f32[256]{0:T(256)S(1)}, f32[256]{0:T(256)S(1)}, f32[1088]{0:T(1024)S(1)}, bf16[1088,256]{1,0:T(8,128)(2,1)}) fusion(f32[1088,256]{1,0:T(8,128)S(1)} %copy-done.3, f32[1088,256]{1,0:T(8,128)S(1)} %copy-done.5, f32[1088]{0:T(1024)S(1)} %get-tuple-element.79, f32[1088,256]{1,0:T(8,128)} %copy-done.8, ...), kind=kLoop, calls=%fused_computation.33 | loop fusion | flops 2782592 | bytes 5028612 | tf_op jit(solution)/shard_map/reduce_sum | solution.py:1259
  157.2 1.6 fusion.74
  158.9 0.1 stack.55
  159.0 0.1 stack.56
  159.1 0.1 stack.57
  159.2 0.2 copy.40
  159.5 1.3 reshape.103
  160.8 0.1 pad.63
  160.9 0.1 pad.76.clone
  161.0 2.1 fusion
  163.1 0.5 copy-done.21
  163.6 1.2 fusion.1
  164.9 0.8 pad_maximum_fusion.1.send
  165.7 0.1 copy-done.6
  165.8 0.2 reshape.105
  166.0 0.9 pad.65.wide
  166.9 0.7 copy.42.bias_ref
  167.6 118.1 %shard_map.256 = (f32[34,4096]{1,0:T(8,128)}, f32[34,4096]{1,0:T(8,128)}, f32[304,384]{1,0:T(8,128)}, f32[304,128]{1,0:T(8,128)}, f32[1,160,256]{2,1,0:T(8,128)}, /*index=5*/f32[48,128]{1,0:T(8,128)}) custom-call(bf16[4,3,1,64,256]{4,3,2,1,0:T(8,128)(2,1)} %pad_maximum_fusion.1.send, s32[1,1024]{1,0:T(1,128)} %constant_dynamic-slice_fusion.2.seg_row_ref, ...), custom_call_target="tpu_custom_call" | custom-call | tf_op jit(solution)/shard_map/pallas_call | solution.py:1189
  285.7 1.0 slice_bitcast_fusion
  286.8 0.7 slice_bitcast_fusion.5
  287.5 0.1 copy.43
  287.6 0.7 pad_maximum_fusion.2
  288.3 1.6 slice_reduce_fusion.3
  289.9 0.6 pad_maximum_fusion.3
  290.5 1.1 dynamic-slice
  291.6 0.7 reshape.108
  292.3 0.8 dynamic-slice_bitcast_fusion
  293.1 0.7 dynamic-slice_bitcast_fusion.1
  293.8 0.7 slice_reduce_fusion.5
  294.5 1.6 slice_reduce_fusion.1
  296.1 0.8 copy.65
  297.0 0.8 copy.66
  (79 shorter events, 0.4 us)
Async XLA Ops:
  0.6 0.7 copy-start
  0.7 3.2 %copy-start.13 = (bf16[34,4096]{1,0:T(8,128)(2,1)S(1)}, bf16[34,4096]{1,0:T(8,128)(2,1)}, u32[]{:S(2)}) copy-start(bf16[34,4096]{1,0:T(8,128)(2,1)} %param.15) | copy-start | bytes 835588
  0.7 4.0 %copy-start.14 = (bf16[34,4096]{1,0:T(8,128)(2,1)S(1)}, bf16[34,4096]{1,0:T(8,128)(2,1)}, u32[]{:S(2)}) copy-start(bf16[34,4096]{1,0:T(8,128)(2,1)} %param.16) | copy-start | bytes 835588
  1.4 4.1 %copy-start.16 = (bf16[272,3,34]{0,2,1:T(8,128)(2,1)S(1)}, bf16[272,3,34]{0,2,1:T(8,128)(2,1)}, u32[]{:S(2)}) copy-start(bf16[272,3,34]{0,2,1:T(8,128)(2,1)} %param.18) | copy-start | bytes 166468
  2.4 3.1 %copy-start.23 = (bf16[136]{0:T(256)(128)(2,1)S(1)}, bf16[136]{0:T(256)(128)(2,1)}, u32[]{:S(2)}) copy-start(bf16[136]{0:T(256)(128)(2,1)} %param.23) | copy-start | bytes 820
  2.4 3.1 %copy-start.15 = (bf16[272,136]{0,1:T(8,128)(2,1)S(1)}, bf16[272,136]{0,1:T(8,128)(2,1)}, u32[]{:S(2)}) copy-start(bf16[272,136]{0,1:T(8,128)(2,1)} %param.22) | copy-start | bytes 221956
  2.4 3.1 %copy-start.18 = (bf16[272,34]{0,1:T(8,128)(2,1)S(1)}, bf16[272,34]{0,1:T(8,128)(2,1)}, u32[]{:S(2)}) copy-start(bf16[272,34]{0,1:T(8,128)(2,1)} %param.20) | copy-start | bytes 55492
  3.8 2.5 slice-start.3
  3.8 2.5 slice-start.2
  131.4 5.5 %slice-start = ((s8[5242880]{0:T(1024)(128)(4,1)}), s8[1048576]{0:T(1024)(128)(4,1)S(1)}, s32[]{:S(2)}) async-start(s8[5242880]{0:T(1024)(128)(4,1)} %bitcast.168), calls=%async_computation | async-start | bytes 2097152
  132.6 4.3 %slice-start.1 = ((s8[5242880]{0:T(1024)(128)(4,1)}), s8[4194304]{0:T(1024)(128)(4,1)S(1)}, s32[]{:S(2)}) async-start(s8[5242880]{0:T(1024)(128)(4,1)} %bitcast.168), calls=%async_computation.1 | async-start | bytes 8388608
  136.9 2.5 copy-start.2
  139.4 1.1 copy-start.4
  139.9 1.5 copy-start.8
  141.9 4.3 %slice-start.4 = ((s8[5308416]{0:T(1024)(128)(4,1)}), s8[4194304]{0:T(1024)(128)(4,1)S(1)}, s32[]{:S(2)}) async-start(s8[5308416]{0:T(1024)(128)(4,1)} %bitcast.193), calls=%async_computation.4 | async-start | bytes 8388608
  142.5 3.7 %slice-start.5 = ((s8[5308416]{0:T(1024)(128)(4,1)}), s8[1114112]{0:T(1024)(128)(4,1)S(1)}, s32[]{:S(2)}) async-start(s8[5308416]{0:T(1024)(128)(4,1)} %bitcast.193), calls=%async_computation.5 | async-start | bytes 2228224
  145.2 1.0 copy-start.9
  148.6 4.3 %copy-start.7 = (f32[1088,16]{1,0:T(8,128)S(1)}, f32[1088,16]{1,0:T(8,128)}, u32[]{:S(2)}) copy-start(f32[1088,16]{1,0:T(8,128)} %get-tuple-element.44) | copy-start | bytes 208900
  148.6 5.4 %copy-start.5 = (f32[1088,256]{1,0:T(8,128)S(1)}, f32[1088,256]{1,0:T(8,128)}, u32[]{:S(2)}) copy-start(f32[1088,256]{1,0:T(8,128)} %get-tuple-element.45) | copy-start | bytes 3342340
  152.9 1.2 copy-start.3
  154.1 3.1 %copy-start.19 = (f32[1,256]{1,0:T(1,128)S(1)}, f32[1,256]{1,0:T(1,128)}, u32[]{:S(2)}) copy-start(f32[1,256]{1,0:T(1,128)} %get-tuple-element.39) | copy-start | bytes 3076
  159.5 1.4 copy-start.20
  159.5 1.5 copy-start.22
  161.0 2.6 copy-start.21
  164.8 1.1 copy-start.6
  165.8 1.1 copy-start.24
  285.7 6.6 %copy-start.12 = (f32[304,384]{1,0:T(8,128)S(1)}, f32[304,384]{1,0:T(8,128)}, u32[]{:S(2)}) copy-start(f32[304,384]{1,0:T(8,128)} %get-tuple-element.56) | copy-start | bytes 1400836
  285.7 8.1 %copy-start.17 = (f32[48,128]{1,0:T(8,128)S(1)}, f32[48,128]{1,0:T(8,128)}, u32[]{:S(2)}) copy-start(f32[48,128]{1,0:T(8,128)} %get-tuple-element.59) | copy-start | bytes 73732
  285.7 10.4 %copy-start.11 = (f32[34,4096]{1,0:T(8,128)S(1)}, f32[34,4096]{1,0:T(8,128)}, u32[]{:S(2)}) copy-start(f32[34,4096]{1,0:T(8,128)} %get-tuple-element.102) | copy-start | bytes 1671172
  290.5 6.5 %copy-start.10 = (f32[34,4096]{1,0:T(8,128)S(1)}, f32[34,4096]{1,0:T(8,128)}, u32[]{:S(2)}) copy-start(f32[34,4096]{1,0:T(8,128)} %get-tuple-element.103) | copy-start | bytes 1671172
  294.5 3.3 %copy-start.1 = (s32[4,1024]{1,0:T(4,128)S(1)}, s32[4,1024]{1,0:T(4,128)}, u32[]{:S(2)}) copy-start(s32[4,1024]{1,0:T(4,128)} %param.17) | copy-start | bytes 49156
